TPU v7x, 768 devices: a whole 4x8x12 slice. The times are simulated.
768 devices in a mesh: group: 16 (over y, core), dom: 48 (over x, z).
Axes of the slice: x: 4, y: 8, z: 12, core: 2. Of those that a mesh axis runs over, the one named last changes fastest.
Arguments:
- features: bfloat16 [196608, 512], P(('group', 'dom')), may hold values from -6 to 6
- cotangent: bfloat16 [196608, 512], P(('group', 'dom')), may hold values from -6 to 6
- w_self: bfloat16 [512, 512], replicated, may hold values from -0.25 to 0.25
- w_neigh: bfloat16 [512, 512], replicated, may hold values from -0.5 to 0.5
- bias: float32 [512], replicated, may hold values from -3 to 3
- neighbours: int32 [196608, 10], P(('group', 'dom')), may hold values from 0 to 3327, as said below
- send_rows: int32 [768, 48, 32], P(('group', 'dom')), may hold values from -1 to 255, as said below
- hub_local: int32 [1536], P(('group', 'dom')), may hold values from 0 to 255, as said below
Outputs:
- output: bfloat16 [196608, 512], P(('group', 'dom'))
- grad_features: float32 [196608, 512], P(('group', 'dom'))
Inputs may be any that keep to these rules, and one draw needn't show every extreme that they name: `send_rows`: row i, peer p: the distinct local rows of device i sent to device p of its group fill the first slots, the rest are -1; a device sends nothing to itself; in every group some device receives 32 rows from each other device of the group, and loads differ widely between receivers. `neighbours`: positions below 256 are own rows; positions 256 + p * 32 + s address only filled slots; positions from 1792 on are hubs, a few hubs far more often than others. `hub_local`: the 2 entries of one device are distinct.
All inputs are finite; a program needn't handle non-finite values.
Results may differ from a plain program's by a relative error of at most 0.0039.
Values may be sent and summed in bfloat16 or wider, within the bound.
A program may use at most 32 MiB of HBM per device.

v0:
```python
import jax
import jax.numpy as jnp
from jax import lax
from jax.sharding import PartitionSpec as P


def tally(neighbours, first, length):
    columns = first + jnp.arange(length, dtype=jnp.int32)

    def add_entry(entry, total):
        picked = lax.dynamic_index_in_dim(neighbours, entry, 1, keepdims=False)
        return total + (picked[:, None] == columns[None, :]).astype(jnp.bfloat16)

    start_total = jnp.zeros((neighbours.shape[0], length), jnp.bfloat16)
    return lax.fori_loop(0, neighbours.shape[1], add_entry, start_total)


def contract_rows(left, right):
    return lax.dot_general(
        left, right, (((0,), (0,)), ((), ())), preferred_element_type=jnp.float32
    )


def body(features, cotangent, w_self, w_neigh, bias, neighbours, send_rows, hub_local):
    vert_rows = features.shape[0]
    fanout = neighbours.shape[1]
    peers = send_rows.shape[1]
    slots = send_rows.shape[2]
    width = features.shape[1]
    hub_dev = hub_local.shape[0]
    hub_total = hub_dev * lax.axis_size(("group", "dom"))
    near_rows = vert_rows + peers * slots
    chosen = send_rows[0]
    filled = chosen >= 0
    safe_rows = jnp.maximum(chosen, 0)
    outgoing = jnp.where(filled[:, :, None], features[safe_rows], jnp.zeros((), jnp.bfloat16))
    arrived = lax.all_to_all(outgoing, "dom", split_axis=0, concat_axis=0, tiled=True)
    near_table = jnp.concatenate([features, arrived.reshape(peers * slots, width)], axis=0)
    counts_near = tally(neighbours, 0, near_rows)
    counts_hub = tally(neighbours, near_rows, hub_total)
    own_hubs = features[hub_local]
    all_hubs = lax.all_gather(own_hubs, ("group", "dom"), axis=0, tiled=True)
    hub_part = jnp.dot(counts_hub, all_hubs, preferred_element_type=jnp.float32)
    agg_sum = jnp.dot(counts_near, near_table, preferred_element_type=jnp.float32) + hub_part
    mean_rows = (agg_sum / fanout).astype(jnp.bfloat16)
    pre = jnp.dot(features, w_self, preferred_element_type=jnp.float32)
    pre = pre + jnp.dot(mean_rows, w_neigh, preferred_element_type=jnp.float32) + bias
    output = jax.nn.silu(pre).astype(jnp.bfloat16)
    sigm = jax.nn.sigmoid(pre)
    grad_pre = (cotangent.astype(jnp.float32) * sigm * (1.0 + pre * (1.0 - sigm))).astype(
        jnp.bfloat16
    )
    flip_dims = (((1,), (1,)), ((), ()))
    grad_self = lax.dot_general(grad_pre, w_self, flip_dims, preferred_element_type=jnp.float32)
    grad_mean = (
        lax.dot_general(grad_pre, w_neigh, flip_dims, preferred_element_type=jnp.float32) / fanout
    ).astype(jnp.bfloat16)
    near_grads = contract_rows(counts_near, grad_mean)
    outgoing_grads = near_grads[vert_rows:].astype(jnp.bfloat16).reshape(peers, slots, width)
    returned = lax.all_to_all(outgoing_grads, "dom", split_axis=0, concat_axis=0, tiled=True)
    every_hub = lax.psum(contract_rows(counts_hub, grad_mean), ("group", "dom"))
    mine = lax.dynamic_slice_in_dim(
        every_hub, lax.axis_index(("group", "dom")) * hub_dev, hub_dev, 0
    )
    grad_features = grad_self + near_grads[:vert_rows]
    targets = jnp.where(filled, chosen, vert_rows).reshape(-1)
    grad_features = grad_features.at[targets].add(
        returned.astype(jnp.float32).reshape(peers * slots, width), mode="drop"
    )
    grad_features = grad_features.at[hub_local].add(mine)
    return (output, grad_features)


def solution(mesh):
    return jax.shard_map(
        body,
        mesh=mesh,
        in_specs=(
            P(("group", "dom"), None),
            P(("group", "dom"), None),
            P(),
            P(),
            P(),
            P(("group", "dom"), None),
            P(("group", "dom"), None, None),
            P(("group", "dom")),
        ),
        out_specs=(P(("group", "dom"), None), P(("group", "dom"), None)),
        check_vma=False,
    )
```

profile of v0, /device:TPU:6, one launch (start us, length us, event | category | flops | bytes accessed | tf_op | source)
XLA Modules:
  0.0 708.3 jit_solution(11594699534425162830)
XLA Ops:
  7.2 0.7 compare_select_fusion.2
  7.9 2.1 gather_fusion.1
  10.1 0.7 broadcast_maximum_fusion
  10.8 0.7 compare_bitcast_fusion
  11.7 5.8 gather_fusion
  17.6 1.4 broadcast_select_fusion
  19.1 18.7 %all-to-all-start = ((bf16[48,32,512]{2,1,0:T(8,128)(2,1)}), bf16[48,32,512]{2,1,0:T(8,128)(2,1)}, u32[]{:S(2)}, u32[]{:S(2)}) async-start(bf16[48,32,512]{2,1,0:T(8,128)(2,1)} %broadcast_select_fusion), calls=%async_computation | async-start | bytes 3145728 | tf_op jit(solution)/shard_map/all_to_all | solution.py:37
  37.8 10.3 %while.29 = (s32[]{:T(128)}, bf16[256,1536]{1,0:T(8,128)(2,1)S(1)}, s32[256,10]{0,1:T(8,128)}, s32[]{:T(128)}, s32[]{:T(128)}) while((s32[]{:T(128)}, bf16[256,1536]{1,0:T(8,128)(2,1)S(1)}, s32[256,10]{0,1:T(8,128)}, s32[]{:T(128)}, s32[]{:T(128)}) %tuple.64), condition=%wide.region_3.4_spmd.clone, body=%wide.region_2.3_spmd.clone.sunk | while | flops 1574403 | bytes 1588299 | solution.py:15
  37.8 0.7 constant_dynamic-slice_fusion.5
  38.5 0.3 fusion.54
  38.8 0.7 constant_dynamic-slice_fusion.5
  39.5 0.3 fusion.54
  39.8 0.7 constant_dynamic-slice_fusion.5
  40.5 0.3 fusion.54
  40.9 0.7 constant_dynamic-slice_fusion.5
  41.6 0.3 fusion.54
  41.9 0.7 constant_dynamic-slice_fusion.5
  42.6 0.3 fusion.54
  42.9 0.7 constant_dynamic-slice_fusion.5
  43.6 0.3 fusion.54
  44.0 0.7 constant_dynamic-slice_fusion.5
  45.0 0.7 constant_dynamic-slice_fusion.5
  45.7 0.3 fusion.54
  46.0 0.7 constant_dynamic-slice_fusion.5
  46.7 0.3 fusion.54
  47.1 0.7 constant_dynamic-slice_fusion.5
  48.1 12.3 %while.28 = (s32[]{:T(128)}, bf16[256,1792]{1,0:T(8,128)(2,1)S(1)}, s32[256,10]{0,1:T(8,128)}, s32[]{:T(128)}, s32[]{:T(128)}) while((s32[]{:T(128)}, bf16[256,1792]{1,0:T(8,128)(2,1)S(1)}, s32[256,10]{0,1:T(8,128)}, s32[]{:T(128)}, s32[]{:T(128)}) %tuple.74), condition=%wide.region_1.2_spmd.clone, body=%wide.region_0.1_spmd.clone.sunk | while | flops 3211267 | bytes 1838155 | solution.py:15
  48.1 0.8 constant_dynamic-slice_fusion.4
  48.9 0.5 fusion.53
  49.4 0.7 constant_dynamic-slice_fusion.4
  50.1 0.5 fusion.53
  50.6 0.7 constant_dynamic-slice_fusion.4
  51.3 0.5 fusion.53
  51.9 0.7 constant_dynamic-slice_fusion.4
  52.6 0.5 fusion.53
  53.1 0.7 constant_dynamic-slice_fusion.4
  53.8 0.5 fusion.53
  54.3 0.7 constant_dynamic-slice_fusion.4
  55.0 0.5 fusion.53
  55.5 0.7 constant_dynamic-slice_fusion.4
  56.2 0.5 fusion.53
  56.7 0.7 constant_dynamic-slice_fusion.4
  57.5 0.5 fusion.53
  58.0 0.7 constant_dynamic-slice_fusion.4
  58.7 0.5 fusion.53
  59.2 0.7 constant_dynamic-slice_fusion.4
  59.9 0.5 fusion.53
  60.7 113.8 %all-gather.4.cloned.1.call-done = bf16[768,2,512]{2,1,0:T(2,128)(2,1)} async-done(((bf16[1,2,512]{2,1,0:T(2,128)(2,1)}), bf16[768,2,512]{2,1,0:T(2,128)(2,1)}) %all-gather.4.cloned.1.call-update) | async-done | bytes 1572880 | tf_op jit(solution)/shard_map/all_gather | solution.py:42
  174.6 3.6 reshape.112
  178.2 2.0 fusion.36
  180.2 3.2 multiply_convert_fusion.1
  183.4 1.5 fusion.23
  184.9 0.7 fusion.37
  185.6 1.8 copy-done.2
  187.4 1.3 slice.17
  188.7 9.7 %all-to-all-start.1 = ((bf16[48,32,512]{2,1,0:T(8,128)(2,1)}), bf16[48,32,512]{2,1,0:T(8,128)(2,1)S(1)}, u32[]{:S(2)}, u32[]{:S(2)}) async-start(bf16[48,32,512]{2,1,0:T(8,128)(2,1)} %bitcast.27), calls=%async_computation.1 | async-start | bytes 3145728 | tf_op jit(solution)/shard_map/all_to_all | solution.py:60
  198.4 2.3 fusion.38
  200.7 0.7 copy-done.5
  201.8 1.7 convolution_add_fusion
  203.4 53.2 %all-to-all-done.1 = bf16[48,32,512]{2,1,0:T(8,128)(2,1)S(1)} async-done(((bf16[48,32,512]{2,1,0:T(8,128)(2,1)}), bf16[48,32,512]{2,1,0:T(8,128)(2,1)S(1)}, u32[]{:S(2)}, u32[]{:S(2)}) %all-to-all-start.1) | async-done | bytes 1572896 | tf_op jit(solution)/shard_map/all_to_all | solution.py:60
  256.6 10.0 %scatter_custom_fusion = f32[256,512]{1,0:T(8,128)S(1)} fusion(f32[256,512]{1,0:T(8,128)S(1)} %convolution_add_fusion, s32[1536]{0:T(1024)S(1)} %fusion.27, bf16[1536,512]{1,0:T(8,128)(2,1)S(1)} %bitcast.26), kind=kCustom, calls=%fused_computation.15 | custom fusion | flops 1572864 | bytes 2097152 | tf_op jit(solution)/shard_map/scatter-add | solution.py:67
  266.6 433.1 %all-reduce.2.cloned.1.call-done = f32[1536,512]{1,0:T(8,128)} async-done(((f32[1536,512]{1,0:T(8,128)}), f32[1536,512]{1,0:T(8,128)}) %all-reduce.2.cloned.1.call-update) | async-done | bytes 3145744 | tf_op jit(solution)/shard_map/psum | solution.py:61
  699.7 1.0 scatter_custom_fusion.1
  700.7 0.8 copy-done.6
  (41 shorter events, 1.7 us)
Async XLA Ops:
  7.2 173.0 %copy-start = (bf16[512,512]{1,0:T(8,128)(2,1)S(1)}, bf16[512,512]{1,0:T(8,128)(2,1)}, u32[]{:S(2)}) copy-start(bf16[512,512]{1,0:T(8,128)(2,1)} %param.15) | copy-start | bytes 1572868
  7.2 167.4 %all-gather.4.cloned.1.call-start = ((), (), s32[]{:S(2)}) async-start(), calls=%async_computation.3 | async-start | bytes 1574912 | tf_op jit(solution)/shard_map/all_gather | solution.py:42
  19.1 161.1 %all-to-all-start = ((bf16[48,32,512]{2,1,0:T(8,128)(2,1)}), bf16[48,32,512]{2,1,0:T(8,128)(2,1)}, u32[]{:S(2)}, u32[]{:S(2)}) async-start(bf16[48,32,512]{2,1,0:T(8,128)(2,1)} %broadcast_select_fusion), calls=%async_computation | async-start | bytes 3145728 | tf_op jit(solution)/shard_map/all_to_all | solution.py:37
  48.1 12.3 %copy-start.1 = (bf16[256,512]{1,0:T(8,128)(2,1)S(1)}, bf16[256,512]{1,0:T(8,128)(2,1)}, u32[]{:S(2)}) copy-start(bf16[256,512]{1,0:T(8,128)(2,1)} %param.12) | copy-start | bytes 786436
  48.1 12.3 %copy-start.3 = (bf16[512,512]{1,0:T(8,128)(2,1)S(1)}, bf16[512,512]{1,0:T(8,128)(2,1)}, u32[]{:S(2)}) copy-start(bf16[512,512]{1,0:T(8,128)(2,1)} %param.14) | copy-start | bytes 1572868
  178.2 2.0 copy-start.7
  185.6 1.8 copy-start.2
  188.7 67.9 %all-to-all-start.1 = ((bf16[48,32,512]{2,1,0:T(8,128)(2,1)}), bf16[48,32,512]{2,1,0:T(8,128)(2,1)S(1)}, u32[]{:S(2)}, u32[]{:S(2)}) async-start(bf16[48,32,512]{2,1,0:T(8,128)(2,1)} %bitcast.27), calls=%async_computation.1 | async-start | bytes 3145728 | tf_op jit(solution)/shard_map/all_to_all | solution.py:60
  198.4 501.3 %all-reduce.2.cloned.1.call-start = ((), (), s32[]{:S(2)}) async-start(), calls=%async_computation.2 | async-start | bytes 6291456 | tf_op jit(solution)/shard_map/psum | solution.py:61
  200.7 0.7 copy-start.5
  200.7 1.1 copy-start.4
  700.7 0.8 copy-start.6
Sparse Core Ops, SparseCore 0:
  14.1 160.3 all-gather.3
  204.6 495.0 all-reduce.1
where the time goes:
time: 710 us; the launch traced here: 708 us
  waiting for transfers between devices  600 us (85%)
  local copies, waits for them, and re-layouts  30.9 us (4%)
  starting transfers between devices  28.4 us (4%)
  other arithmetic  22.6 us (3%)
  between operations  14.2 us (2%)
  matrix products  11.6 us (2%)
    psum x1, waiting for transfers between devices, body(): every_hub = lax.psum(contract_rows(counts_hub, grad_mean), ('group', 'dom'))  433 us
    all_gather x1, waiting for transfers between devices, body(): all_hubs = lax.all_gather(own_hubs, ('group', 'dom'), axis=0, tiled=True)  114 us
    all_to_all x1, waiting for transfers between devices, body(): lax.all_to_all(outgoing_grads, 'dom', split_axis=0, concat_axis=0, tiled=...  53.2 us
    all_to_all x1, starting transfers between devices, body(): lax.all_to_all(outgoing, 'dom', split_axis=0, concat_axis=0, tiled=True)  18.7 us
  transfers between devices with their start and end apart: 4, of which 3 were waited for; matrix products, arithmetic and copies ran while one was open for 7% of the time, Pallas kernels for 0%

commit v1 on v0

v1 whole, which is shorter than its diff:
```python
import functools

import jax
import jax.numpy as jnp
from jax import lax
from jax.experimental import pallas as pl
from jax.experimental.pallas import tpu as pltpu
from jax.sharding import PartitionSpec as P

ZN = 12
F32 = jnp.float32
BF16 = jnp.bfloat16


def dot_t(left, right):
    return lax.dot_general(left, right, (((0,), (0,)), ((), ())), preferred_element_type=F32)


def dot_b(left, right):
    return lax.dot_general(left, right, (((1,), (1,)), ((), ())), preferred_element_type=F32)


def dot(left, right):
    return jnp.dot(left, right, preferred_element_type=F32)


def kernel(
    yn, xn, zn, feat, cot, ws, wn, bias, nbrt, lst, hubl, out, gout,
    tab, sel, orow, arr, grow, ret, hubtab,
    ha_s, ha, hb_s, hb, hubg, sib, ysr, yrr, ysl, yrl, xb_s, xb, za_s, za,
    sem_a2a, sem_ha, sem_hb, sem_yr, sem_yl, sem_sib, sem_sibg, sem_gr, sem_gl, sem_xb, sem_za,
):
    verts, width = feat.shape
    fanout = nbrt.shape[0]
    peers, slots = arr.shape[0], arr.shape[1]
    lanes = 128
    quarter = width // lanes
    near = peers * slots
    group = lax.axis_index("group")
    dom = lax.axis_index("dom")
    y, core = group // 2, lax.rem(group, 2)
    x, z = dom // zn, lax.rem(dom, zn)
    half_y = yn // 2

    def up(step):
        return lax.rem(y + step + 2 * yn, yn)

    def copy(src, dst, sems, at, **to):
        return pltpu.make_async_remote_copy(
            src_ref=src, dst_ref=dst, send_sem=sems.at[(0,) + at], recv_sem=sems.at[(1,) + at],
            device_id=to, device_id_type=pl.DeviceIdType.MESH,
        )

    right = {"group": up(1) * 2 + core}
    left = {"group": up(-1) * 2 + core}
    sibling = {"group": y * 2 + 1 - core}

    barrier = pltpu.get_barrier_semaphore()

    def greet(i, carry):
        pl.semaphore_signal(barrier, 1, device_id={"dom": lax.rem(dom + i, peers)}, device_id_type=pl.DeviceIdType.MESH)
        return carry

    lax.fori_loop(1, peers, greet, 0)
    for partner in (right, left, sibling):
        pl.semaphore_signal(barrier, 1, device_id=partner, device_id_type=pl.DeviceIdType.MESH)

    row_id = lax.broadcasted_iota(jnp.int32, (16, verts), 0)
    vert_id = lax.broadcasted_iota(jnp.int32, (16, verts), 1)
    hub0, hub1 = hubl[0], hubl[1]
    wanted = jnp.where(row_id == 0, hub0, jnp.where(row_id == 1, hub1, -1))
    hub_rows = dot((vert_id == wanted).astype(BF16), feat[...])
    for q in range(quarter):
        ha_s[2 * q:2 * q + 2, :] = hub_rows[0:2, q * lanes:(q + 1) * lanes]
    ha[z] = ha_s[...]

    pl.semaphore_wait(barrier, peers + 2)

    def send_ha(i):
        to = lax.rem(z + i, zn)
        return copy(ha_s, ha.at[z], sem_ha, (i,), dom=x * zn + to)

    def loop(lo, hi, body):
        lax.fori_loop(lo, hi, lambda i, c: (body(i), c)[1], 0)

    loop(1, zn, lambda i: send_ha(i).start())

    chunks = lst.shape[0]
    per = peers // chunks
    sub_id = lax.broadcasted_iota(jnp.int32, (verts, lanes), 0)

    def pick(c):
        chosen = (sub_id == lst[pl.ds(c, 1), :]).astype(BF16)
        sel[c] = chosen
        rows = dot_t(chosen, feat[...]).astype(BF16)
        orow[pl.ds(c * per, per)] = rows.reshape(per, slots, width)

    loop(0, chunks, pick)
    arr[dom] = jnp.zeros((slots, width), BF16)
    ret[dom] = jnp.zeros((slots, width), BF16)

    def all_to_all(src, dst, way):
        def send(i):
            to = lax.rem(dom + 7 * i, peers)
            copy(src.at[to], dst.at[dom], sem_a2a, (way,), dom=to).start()

        loop(1, peers, send)

    def all_to_all_wait(src, dst, way):
        some = pl.ds(0, peers - 1)
        done = pltpu.make_async_remote_copy(
            src_ref=src.at[some], dst_ref=dst.at[some], send_sem=sem_a2a.at[0, way], recv_sem=sem_a2a.at[1, way],
            device_id={"dom": lax.rem(dom + 1, peers)}, device_id_type=pl.DeviceIdType.MESH,
        )
        done.wait()

    all_to_all(orow, arr, 0)

    loop(1, zn, lambda i: send_ha(i).wait())
    for zz in range(zn):
        for q in range(quarter):
            hb_s[2 * zz:2 * zz + 2, q * lanes:(q + 1) * lanes] = ha[zz, 2 * q:2 * q + 2, :]
    hb[x] = hb_s[...]

    def send_hb(i):
        return copy(hb_s, hb.at[x], sem_hb, (i,), dom=lax.rem(x + i, xn) * zn + z)

    for i in range(1, xn):
        send_hb(i).start()

    tall = 128

    def tally(i):
        rows = lax.broadcasted_iota(jnp.int32, (tall, verts), 0) + i * tall
        total = jnp.zeros((tall, verts), F32)
        for e in range(fanout):
            total = jnp.where(nbrt[e:e + 1, :] == rows, total + 1.0, total)
        tab[pl.ds(pl.multiple_of(i * tall, tall), tall), :] = total.astype(BF16)

    tiles = tab.shape[0] // tall
    cuts = [tiles * k // (half_y + 2) for k in range(half_y + 3)]
    loop(cuts[0], cuts[1], tally)

    for i in range(1, xn):
        send_hb(i).wait()
    block = hubtab.shape[1]
    hubtab[group] = hb[...].reshape(block, width).astype(BF16)

    def send_y(way, step):
        sems, owner, to = (sem_yr, up(1 - step), right) if way > 0 else (sem_yl, up(step - 1), left)
        part = hubtab.at[owner * 2 + core]
        if step == half_y:
            part = part.at[pl.ds(0 if way > 0 else block // 2, block // 2)]
        return copy(part, part, sems, (step,), **to)

    def send_sib(at, owner_y):
        part = hubtab.at[owner_y * 2 + core]
        return copy(part, part, sem_sib, (at,), **sibling)

    send_sib(0, y).start()
    send_y(1, 1).start()
    send_y(-1, 1).start()
    for step in range(1, half_y + 1):
        loop(cuts[step], cuts[step + 1], tally)
        send_y(1, step).wait_recv()
        send_y(-1, step).wait_recv()
        if step < half_y:
            send_y(1, step + 1).start()
            send_y(-1, step + 1).start()
            send_sib(2 * step - 1, up(-step)).start()
            send_sib(2 * step, up(step)).start()
        else:
            send_sib(2 * step - 1, up(step)).start()
    loop(cuts[half_y + 1], cuts[half_y + 2], tally)
    for step in range(1, half_y + 1):
        send_y(1, step).wait_send()
        send_y(-1, step).wait_send()

    hub_at = verts + near
    agg = dot_t(tab[0:verts, :], feat[...])
    pre = dot(feat[...], ws[...]) + bias[...]
    for i in range(yn):
        send_sib(i, y).wait()
    agg += dot_t(tab[hub_at:, :], hubtab[...].reshape(2 * yn * block, width))
    all_to_all_wait(orow, arr, 0)
    agg += dot_t(tab[verts:hub_at, :], arr[...].reshape(near, width))

    mean = (agg / fanout).astype(BF16)
    pre += dot(mean, wn[...])
    sigm = jax.nn.sigmoid(pre)
    out[...] = (pre * sigm).astype(BF16)
    grad_pre = (cot[...].astype(F32) * sigm * (1.0 + pre * (1.0 - sigm))).astype(BF16)
    grad_mean = (dot_b(grad_pre, wn[...]) / fanout).astype(BF16)

    grow[...] = dot(tab[verts:hub_at, :], grad_mean).astype(BF16).reshape(peers, slots, width)
    all_to_all(grow, ret, 1)

    hubg[...] = dot(tab[hub_at:, :], grad_mean).reshape(2 * yn, block, width)

    def send_sibg(i):
        owner = up(i)
        return copy(hubg.at[owner * 2 + 1 - core], sib.at[owner], sem_sibg, (i,), **sibling)

    order = [half_y]
    for i in range(half_y - 1, 0, -1):
        order += [i, yn - i]
    order += [0]
    for i in order:
        send_sibg(i).start()
    gout[...] = dot(tab[0:verts, :], grad_mean) + dot_b(grad_pre, ws[...])

    def mine(step):
        owner = up(step)
        return hubg[owner * 2 + core] + sib[owner]

    def send_g(way, k):
        sems, src, dst, to = (sem_gr, ysr, yrr, right) if way > 0 else (sem_gl, ysl, yrl, left)
        src, dst = src.at[k], dst.at[k]
        if k == half_y:
            part = pl.ds(0 if way > 0 else block // 2, block // 2)
            src, dst = src.at[part], dst.at[part]
        return copy(src, dst, sems, (k,), **to)

    lower, upper = slice(0, block // 2), slice(block // 2, block)
    send_sibg(half_y).wait_recv()
    far = mine(half_y)
    ysr[half_y, lower] = far[lower]
    ysl[half_y, upper] = far[upper]
    send_g(1, half_y).start()
    send_g(-1, half_y).start()
    for k in range(half_y - 1, -1, -1):
        for i in sorted({k, (yn - k) % yn}):
            send_sibg(i).wait_recv()
        send_g(1, k + 1).wait_recv()
        send_g(-1, k + 1).wait_recv()
        if k == half_y - 1:
            if k > 0:
                on_r, on_l = mine(k), mine(-k)
                ysr[k, lower] = on_r[lower] + yrr[k + 1, lower]
                ysr[k, upper] = on_r[upper]
                ysl[k, lower] = on_l[lower]
                ysl[k, upper] = on_l[upper] + yrl[k + 1, upper]
            else:
                total = mine(0)
                ysr[0, lower] = total[lower] + yrr[1, lower]
                ysr[0, upper] = total[upper] + yrl[1, upper]
        elif k > 0:
            ysr[k] = mine(k) + yrr[k + 1]
            ysl[k] = mine(-k) + yrl[k + 1]
        else:
            ysr[0] = mine(0) + yrr[1] + yrl[1]
        if k > 0:
            send_g(1, k).start()
            send_g(-1, k).start()
    xb_s[...] = ysr[0].reshape(xn, 2 * zn, width)

    def send_xb(i):
        to = lax.rem(x + i, xn)
        return copy(xb_s.at[to], xb.at[i], sem_xb, (i,), dom=to * zn + z)

    for i in range(1, xn):
        send_xb(i).start()
    total = xb_s[x]
    for i in range(1, xn):
        send_xb(i).wait_recv()
        total = total + xb[i]
    for zz in range(zn):
        for q in range(quarter):
            za_s[zz, 2 * q:2 * q + 2, :] = total[2 * zz:2 * zz + 2, q * lanes:(q + 1) * lanes]

    def send_za(i):
        to = lax.rem(z + i, zn)
        return copy(za_s.at[to], za.at[i], sem_za, (i,), dom=x * zn + to)

    loop(1, zn, lambda i: send_za(i).start())
    all_to_all_wait(grow, ret, 1)

    def back(c):
        rows = ret[pl.ds(c * per, per)].reshape(lanes, width)
        gout[...] += dot(sel[c], rows)

    loop(0, chunks, back)
    loop(1, zn, lambda i: send_za(i).wait_recv())
    za[0] = za_s[z]
    hub_sum = za[0]
    for i in range(1, zn):
        hub_sum = hub_sum + za[i]
    rows_of = lax.broadcasted_iota(jnp.int32, (verts, lanes), 0)
    for q in range(quarter):
        cols = slice(q * lanes, (q + 1) * lanes)
        gout[:, cols] += jnp.where(rows_of == hub0, hub_sum[2 * q:2 * q + 1], 0.0) + jnp.where(
            rows_of == hub1, hub_sum[2 * q + 1:2 * q + 2], 0.0
        )

    for i in range(yn):
        send_sibg(i).wait_send()
    for k in range(1, half_y + 1):
        send_g(1, k).wait_send()
        send_g(-1, k).wait_send()
    for i in range(1, xn):
        send_xb(i).wait_send()
    loop(1, zn, lambda i: send_za(i).wait_send())


def body(features, cotangent, w_self, w_neigh, bias, neighbours, send_rows, hub_local):
    verts, width = features.shape
    peers, slots = send_rows.shape[1:]
    xn, zn = peers // ZN, ZN
    groups = lax.axis_size("group")
    yn = groups // 2
    half_y = yn // 2
    near = peers * slots
    block = 2 * peers
    lst = send_rows.reshape(near // 128, 128)
    vmem = pl.BlockSpec(memory_space=pltpu.VMEM)
    dma = pltpu.SemaphoreType.DMA
    return pl.pallas_call(
        functools.partial(kernel, yn, xn, zn),
        out_shape=(
            jax.ShapeDtypeStruct((verts, width), BF16),
            jax.ShapeDtypeStruct((verts, width), F32),
        ),
        in_specs=[vmem] * 7 + [pl.BlockSpec(memory_space=pltpu.SMEM)],
        out_specs=(vmem, vmem),
        scratch_shapes=[
            pltpu.VMEM((verts + near + groups * block, verts), BF16),
            pltpu.VMEM((near // 128, verts, 128), BF16),
            pltpu.VMEM((peers, slots, width), BF16),
            pltpu.VMEM((peers, slots, width), BF16),
            pltpu.VMEM((peers, slots, width), BF16),
            pltpu.VMEM((peers, slots, width), BF16),
            pltpu.VMEM((groups, block, width), BF16),
            pltpu.VMEM((width // 64, 128), F32),
            pltpu.VMEM((zn, width // 64, 128), F32),
            pltpu.VMEM((2 * zn, width), F32),
            pltpu.VMEM((xn, 2 * zn, width), F32),
            pltpu.VMEM((groups, block, width), F32),
            pltpu.VMEM((yn, block, width), F32),
            pltpu.VMEM((half_y + 1, block, width), F32),
            pltpu.VMEM((half_y + 1, block, width), F32),
            pltpu.VMEM((half_y + 1, block, width), F32),
            pltpu.VMEM((half_y + 1, block, width), F32),
            pltpu.VMEM((xn, 2 * zn, width), F32),
            pltpu.VMEM((xn, 2 * zn, width), F32),
            pltpu.VMEM((zn, width // 64, 128), F32),
            pltpu.VMEM((zn, width // 64, 128), F32),
            dma((2, 2)),
            dma((2, zn)),
            dma((2, xn)),
            dma((2, half_y + 1)),
            dma((2, half_y + 1)),
            dma((2, yn)),
            dma((2, yn)),
            dma((2, half_y + 1)),
            dma((2, half_y + 1)),
            dma((2, xn)),
            dma((2, zn)),
        ],
        compiler_params=pltpu.CompilerParams(
            collective_id=0, has_side_effects=True, vmem_limit_bytes=56 * 1024 * 1024
        ),
    )(features, cotangent, w_self, w_neigh, bias.reshape(1, width), neighbours.T, lst, hub_local)


def solution(mesh):
    rows = P(("group", "dom"), None)
    return jax.shard_map(
        body,
        mesh=mesh,
        in_specs=(rows, rows, P(), P(), P(), rows, P(("group", "dom"), None, None), P(("group", "dom"))),
        out_specs=(rows, rows),
        check_vma=False,
    )
```

time: 710 us -> 142 us (0.20)
  waiting for transfers between devices: 600 us -> 0 us
  Pallas kernels: 0 us -> 136 us
  starting transfers between devices: 28.4 us -> 0 us
  local copies, waits for them, and re-layouts: 30.9 us -> 3.99 us
  other arithmetic: 22.6 us -> 0 us
  between operations: 14.2 us -> 0.65 us
  matrix products: 11.6 us -> 0 us
    psum x1 -> x0, waiting for transfers between devices: 433 us -> none  [body(): every_hub = lax.psum(contract_rows(counts_hub, grad_mean), ('group', 'dom'))]
    pallas_call x0 -> x1, Pallas kernels: none -> 136 us  [body(): pl.pallas_call(functools.partial(kernel, yn, xn, zn), out_shape=(jax.Shap...]
    all_gather x1 -> x0, waiting for transfers between devices: 114 us -> none  [body(): all_hubs = lax.all_gather(own_hubs, ('group', 'dom'), axis=0, tiled=True)]
    all_to_all x2 -> x0, waiting for transfers between devices: 53.2 us -> none  [the longest x1 53.2 us: body(): lax.all_to_all(outgoing_grads, 'dom', split_axis=0, concat_axis=0, tiled=...]
    all_to_all x2 -> x0, starting transfers between devices: 28.4 us -> none  [the longest x1 18.7 us: body(): lax.all_to_all(outgoing, 'dom', split_axis=0, concat_axis=0, tiled=True)]
    dynamic_slice x20 -> x0, local copies, waits for them, and re-layouts: 14.2 us -> none  [add_entry(): picked = lax.dynamic_index_in_dim(neighbours, entry, 1, keepdims=False)]
    dot_general x7 -> x0, matrix products: 11.6 us -> none  [the longest x1 3.19 us: body(): jnp.dot(mean_rows, w_neigh, preferred_element_type=jnp.float32)]
    scatter-add x2 -> x0, other arithmetic: 11 us -> none  [the longest x1 9.99 us: body(): grad_features.at[targets]]
  transfers between devices with their start and end apart: 4 -> 0, of which waited for: 3 -> 0; matrix products, arithmetic and copies ran while one was open for 7% -> 0% of each run, Pallas kernels for 0% -> 0%
where the time goes in v1:
time: 142 us; the launch traced here: 141 us
  Pallas kernels  136 us (96%)
  local copies, waits for them, and re-layouts  3.99 us (3%)
    pallas_call x1, Pallas kernels, body(): pl.pallas_call(functools.partial(kernel, yn, xn, zn), out_shape=(jax.Shap...  136 us
    unnamed x5, local copies, waits for them, and re-layouts  3.32 us

profile of v1, /device:TPU:6, one launch (start us, length us, event | category | flops | bytes accessed | tf_op | source)
XLA Modules:
  0.0 141.0 jit_solution(13076285234741941877)
XLA Ops:
  0.6 0.8 copy.11
  1.4 0.7 reshape.11.lst
  2.1 136.4 %shard_map.95 = (bf16[256,512]{1,0:T(8,128)(2,1)}, f32[256,512]{1,0:T(8,128)}) custom-call(bf16[256,512]{1,0:T(8,128)(2,1)} %feat.1, bf16[256,512]{1,0:T(8,128)(2,1)} %cot.1, bf16[512,512]{1,0:T(8,128)(2,1)} %ws.1, bf16[512,512]{1,0:T(8,128)(2,1)} %wn.1, f32[1,512]{1,0:T(1,128)} %bitcast.3, s32[10,256]{1,0:T(8,128)} %bitcast.2, s32[12,128]{1,0:T(8,128)} %reshape.11.lst, ...), custom_call_target="tpu_custom_call" | custom-call | tf_op jit(solution)/shard_map/pallas_call | solution.py:317
  138.5 0.0 copy-start
  138.5 1.7 %copy.14 = bf16[256,512]{1,0:T(8,128)(2,1)} copy(bf16[256,512]{1,0:T(8,128)(2,1)} %get-tuple-element.4) | data formatting | bytes 524288
  140.2 0.0 copy-done
  140.3 0.8 copy.15
Async XLA Ops:
  138.5 1.7 %copy-start = (f32[256,512]{1,0:T(8,128)S(1)}, f32[256,512]{1,0:T(8,128)}, u32[]{:S(2)}) copy-start(f32[256,512]{1,0:T(8,128)} %get-tuple-element.5) | copy-start | bytes 1572868

commit v2 on v1

v2 whole, which is shorter than its diff:
```python
import functools

import jax
import jax.numpy as jnp
from jax import lax
from jax.experimental import pallas as pl
from jax.experimental.pallas import tpu as pltpu
from jax.sharding import PartitionSpec as P

ZN = 12
F32 = jnp.float32
BF16 = jnp.bfloat16


def dot_t(left, right):
    return lax.dot_general(left, right, (((0,), (0,)), ((), ())), preferred_element_type=F32)


def dot_b(left, right):
    return lax.dot_general(left, right, (((1,), (1,)), ((), ())), preferred_element_type=F32)


def dot(left, right):
    return jnp.dot(left, right, preferred_element_type=F32)


def kernel(
    yn, xn, zn, feat, cot, ws, wn, bias, nbrt, lst, hubl, out, gout,
    tab, sel, zrows, xsend, arr, gsend, gback, zout, zin, hubtab,
    ha_s, ha, hb_s, hb, hubg, sib, ysr, yrr, ysl, yrl, xb_s, xb, za_s, za,
    sem_z, sem_rz, sem_x, sem_xg, sem_ha, sem_hb, sem_y, sem_sib, sem_sibg, sem_ry, sem_xb, sem_za,
):
    verts, width = feat.shape
    fanout = nbrt.shape[0]
    slots = arr.shape[2]
    lanes = 128
    tall = xn * slots
    quarter = width // lanes
    near = zn * tall
    hub_at = verts + near
    group = lax.axis_index("group")
    dom = lax.axis_index("dom")
    y, core = group // 2, lax.rem(group, 2)
    x, z = dom // zn, lax.rem(dom, zn)
    half_y, half_z = yn // 2, zn // 2
    cut = verts // 2

    def up_y(step):
        return lax.rem(y + step + 2 * yn, yn)

    def up_z(step):
        return lax.rem(z + step + 2 * zn, zn)

    def copy(src, dst, sems, at, **to):
        return pltpu.make_async_remote_copy(
            src_ref=src, dst_ref=dst, send_sem=sems.at[(0,) + at], recv_sem=sems.at[(1,) + at],
            device_id=to, device_id_type=pl.DeviceIdType.MESH,
        )

    def loop(lo, hi, body):
        lax.fori_loop(lo, hi, lambda i, c: (body(i), c)[1], 0)

    y_next = {1: {"group": up_y(1) * 2 + core}, -1: {"group": up_y(-1) * 2 + core}}
    z_next = {1: {"dom": x * zn + up_z(1)}, -1: {"dom": x * zn + up_z(-1)}}
    sibling = {"group": y * 2 + 1 - core}

    barrier = pltpu.get_barrier_semaphore()

    def greet(**to):
        pl.semaphore_signal(barrier, 1, device_id=to, device_id_type=pl.DeviceIdType.MESH)

    loop(1, zn, lambda i: greet(dom=x * zn + up_z(i)))
    for i in range(1, xn):
        greet(dom=lax.rem(x + i, xn) * zn + z)
    for partner in (y_next[1], y_next[-1], sibling):
        greet(**partner)

    row_id = lax.broadcasted_iota(jnp.int32, (16, verts), 0)
    vert_id = lax.broadcasted_iota(jnp.int32, (16, verts), 1)
    hub0, hub1 = hubl[0], hubl[1]
    wanted = jnp.where(row_id == 0, hub0, jnp.where(row_id == 1, hub1, -1))
    hub_rows = dot((vert_id == wanted).astype(BF16), feat[...])
    tile = 2 * quarter
    for zz in range(zn):
        for q in range(quarter):
            ha_s[zz, 2 * q:2 * q + 2, :] = hub_rows[0:2, q * lanes:(q + 1) * lanes]
        ha_s[zz, tile:tile + 8, :] = jnp.broadcast_to(lst[zz:zz + 1, :], (8, tall))
    ha[z] = ha_s[z]

    def tally(i):
        sub = lax.broadcasted_iota(jnp.int32, (tall, verts), 0)
        at = i * tall
        zz = i - verts // tall
        border = verts + zz * slots + (sub // slots) * (zn * slots) + lax.rem(sub, slots)
        is_border = jnp.logical_and(zz >= 0, zz < zn)
        rows = jnp.where(is_border, border, at + sub)
        total = jnp.zeros((tall, verts), F32)
        for e in range(fanout):
            total = jnp.where(nbrt[e:e + 1, :] == rows, total + 1.0, total)
        tab[pl.ds(pl.multiple_of(at, tall), tall), :] = total.astype(BF16)

    tiles = tab.shape[0] // tall
    spots = 2 * half_z + 1
    cuts = [tiles * k // spots for k in range(spots + 1)]

    def tally_part(k):
        loop(cuts[k], cuts[k + 1], tally)

    tally_part(0)
    pl.semaphore_wait(barrier, zn - 1 + xn - 1 + 3)

    def send_z(way, hop, part):
        owner = up_z(way * (1 - hop))
        rows = pl.ds(part * cut, cut)
        src = feat if hop == 1 else zrows.at[owner]
        return copy(src.at[rows], zrows.at[owner, rows], sem_z, (way + 1, hop, part), **z_next[way])

    def goes(way, hop, part):
        return hop < half_z or (hop == half_z and part == (0 if way > 0 else 1))

    def send_ha(i):
        to = up_z(i)
        return copy(ha_s.at[to], ha.at[z], sem_ha, (i,), dom=x * zn + to)

    loop(1, zn, lambda i: send_ha(i).start())
    for part, way in ((0, 1), (1, -1), (1, 1), (0, -1)):
        if goes(way, 1, part):
            send_z(way, 1, part).start()

    sub_id = lax.broadcasted_iota(jnp.int32, (verts, tall), 0).astype(F32)

    def pick(zz, rows):
        chosen = (sub_id == ha[zz, tile:tile + 1, :]).astype(BF16)
        sel[zz] = chosen
        xsend[zz] = dot_t(chosen, rows).astype(BF16).reshape(xn, slots, width)
        arr[zz, x] = xsend[zz, x]
        for i in range(1, xn):
            to = lax.rem(x + i, xn)
            copy(xsend.at[zz, to], arr.at[zz, x], sem_x, (0,), dom=to * zn + z).start()

    def hub_z():
        loop(1, zn, lambda i: send_ha(i).wait())
        for zz in range(zn):
            for q in range(quarter):
                hb_s[2 * zz:2 * zz + 2, q * lanes:(q + 1) * lanes] = ha[zz, 2 * q:2 * q + 2, :]
        hb[x] = hb_s[...]
        for i in range(1, xn):
            send_hb(i).start()

    def send_hb(i):
        return copy(hb_s, hb.at[x], sem_hb, (i,), dom=lax.rem(x + i, xn) * zn + z)

    block = hubtab.shape[1]

    def send_y(way, hop):
        owner = up_y(way * (1 - hop))
        part = hubtab.at[owner * 2 + core]
        if hop == half_y:
            part = part.at[pl.ds(0 if way > 0 else block // 2, block // 2)]
        return copy(part, part, sem_y, (way + 1, hop), **y_next[way])

    def send_sib(at, owner_y):
        part = hubtab.at[owner_y * 2 + core]
        return copy(part, part, sem_sib, (at,), **sibling)

    def hub_x():
        for i in range(1, xn):
            send_hb(i).wait()
        hubtab[group] = hb[...].reshape(block, width).astype(BF16)
        send_y(1, 1).start()
        send_y(-1, 1).start()
        send_sib(0, y).start()

    def hub_y(hop):
        send_y(1, hop).wait_recv()
        send_y(-1, hop).wait_recv()
        if hop < half_y:
            send_y(1, hop + 1).start()
            send_y(-1, hop + 1).start()
            send_sib(2 * hop - 1, up_y(-hop)).start()
            send_sib(2 * hop, up_y(hop)).start()
        else:
            send_sib(2 * hop - 1, up_y(hop)).start()

    hub_steps = [hub_z, hub_x] + [functools.partial(hub_y, hop) for hop in range(1, half_y + 1)]
    spot = 0
    for hop in range(1, half_z + 1):
        for turn, pair in enumerate((((1, 0), (-1, 1)), ((1, 1), (-1, 0)))):
            for way, part in pair:
                if goes(way, hop, part):
                    send_z(way, hop, part).wait_recv()
                    if goes(way, hop + 1, part):
                        send_z(way, hop + 1, part).start()
            if turn == 0:
                if hop == 1:
                    pick(z, feat[...])
                else:
                    pick(up_z(1 - hop), zrows[up_z(1 - hop)])
            elif hop > 1:
                pick(up_z(hop - 1), zrows[up_z(hop - 1)])
            if hub_steps:
                hub_steps.pop(0)()
            spot += 1
            tally_part(spot)
    pick(up_z(half_z), zrows[up_z(half_z)])
    while hub_steps:
        hub_steps.pop(0)()

    agg = dot_t(tab[0:verts, :], feat[...])
    pre = dot(feat[...], ws[...]) + bias[...]
    for i in range(yn):
        send_sib(i, y).wait()
    agg += dot_t(tab[hub_at:, :], hubtab[...].reshape(2 * yn * block, width))
    if xn > 1:
        most = (pl.ds(0, zn), pl.ds(0, xn - 1))
        copy(xsend.at[most], arr.at[most], sem_x, (0,), dom=lax.rem(x + 1, xn) * zn + z).wait()
    agg += dot_t(tab[verts:hub_at, :], arr[...].reshape(near, width))

    mean = (agg / fanout).astype(BF16)
    pre += dot(mean, wn[...])
    sigm = jax.nn.sigmoid(pre)
    out[...] = (pre * sigm).astype(BF16)
    grad_pre = (cot[...].astype(F32) * sigm * (1.0 + pre * (1.0 - sigm))).astype(BF16)
    grad_mean = (dot_b(grad_pre, wn[...]) / fanout).astype(BF16)

    def give(t):
        j = lax.rem(jnp.where(lax.rem(t, 2) == 1, half_z - (t + 1) // 2, t // 2 - half_z) + zn, zn)
        zz = up_z(j)
        rows = pl.ds(pl.multiple_of(verts + zz * tall, tall), tall)
        gsend[zz] = dot(tab[rows, :], grad_mean).astype(BF16).reshape(xn, slots, width)
        gback[zz, x] = gsend[zz, x]
        for i in range(1, xn):
            to = lax.rem(x + i, xn)
            copy(gsend.at[zz, to], gback.at[zz, x], sem_xg, (j,), dom=to * zn + z).start()

    loop(0, zn, give)
    hubg[...] = dot(tab[hub_at:, :], grad_mean).reshape(2 * yn, block, width)

    def send_sibg(i):
        owner = up_y(i)
        return copy(hubg.at[owner * 2 + 1 - core], sib.at[owner], sem_sibg, (i,), **sibling)

    order = [half_y]
    for i in range(half_y - 1, 0, -1):
        order += [i, yn - i]
    order += [0]
    for i in order:
        send_sibg(i).start()

    def given(j):
        some = pl.ds(0, xn - 1)
        zz = up_z(j)
        return copy(gsend.at[zz, some], gback.at[zz, some], sem_xg, (j % zn,), dom=lax.rem(x + 1, xn) * zn + z)

    def owed(j):
        if xn > 1:
            given(j).wait_recv()
        zz = up_z(j)
        return dot(sel[zz], gback[zz].reshape(tall, width))

    def send_g(way, hop, part):
        at, rows = (way + 1) // 2, pl.ds(part * cut, cut)
        return copy(zout.at[at, hop, rows], zin.at[at, hop, rows], sem_rz, (way + 1, hop, part), **z_next[way])

    def start_z():
        far = owed(half_z)
        for way, part in ((1, 0), (-1, 1)):
            rows = slice(part * cut, (part + 1) * cut)
            zout[(way + 1) // 2, half_z, rows] = far[rows].astype(BF16)
            send_g(way, half_z, part).start()

    def step_z(hop):
        terms = {1: owed(hop), -1: owed(-hop)}
        for way, part in ((1, 1), (-1, 0), (1, 0), (-1, 1)):
            rows = slice(part * cut, (part + 1) * cut)
            value = terms[way][rows]
            if goes(way, hop + 1, part):
                send_g(way, hop + 1, part).wait_recv()
                value = value + zin[(way + 1) // 2, hop + 1, rows].astype(F32)
            zout[(way + 1) // 2, hop, rows] = value.astype(BF16)
            send_g(way, hop, part).start()

    def mine(step):
        owner = up_y(step)
        return hubg[owner * 2 + core] + sib[owner]

    def send_h(way, k):
        src, dst = (ysr, yrr) if way > 0 else (ysl, yrl)
        src, dst = src.at[k], dst.at[k]
        if k == half_y:
            part = pl.ds(0 if way > 0 else block // 2, block // 2)
            src, dst = src.at[part], dst.at[part]
        return copy(src, dst, sem_ry, (way + 1, k), **y_next[way])

    lower, upper = slice(0, block // 2), slice(block // 2, block)

    def start_y():
        send_sibg(half_y).wait_recv()
        far = mine(half_y)
        ysr[half_y, lower] = far[lower]
        ysl[half_y, upper] = far[upper]
        send_h(1, half_y).start()
        send_h(-1, half_y).start()

    def step_y(k):
        for i in sorted({k, (yn - k) % yn}):
            send_sibg(i).wait_recv()
        send_h(1, k + 1).wait_recv()
        send_h(-1, k + 1).wait_recv()
        if k == half_y - 1:
            if k > 0:
                on_r, on_l = mine(k), mine(-k)
                ysr[k, lower] = on_r[lower] + yrr[k + 1, lower]
                ysr[k, upper] = on_r[upper]
                ysl[k, lower] = on_l[lower]
                ysl[k, upper] = on_l[upper] + yrl[k + 1, upper]
            else:
                total = mine(0)
                ysr[0, lower] = total[lower] + yrr[1, lower]
                ysr[0, upper] = total[upper] + yrl[1, upper]
        elif k > 0:
            ysr[k] = mine(k) + yrr[k + 1]
            ysl[k] = mine(-k) + yrl[k + 1]
        else:
            ysr[0] = mine(0) + yrr[1] + yrl[1]
        if k > 0:
            send_h(1, k).start()
            send_h(-1, k).start()

    def send_xb(i):
        to = lax.rem(x + i, xn)
        return copy(xb_s.at[to], xb.at[i], sem_xb, (i,), dom=to * zn + z)

    def send_za(i):
        to = up_z(i)
        return copy(za_s.at[to], za.at[i], sem_za, (i,), dom=x * zn + to)

    def start_x():
        xb_s[...] = ysr[0].reshape(xn, 2 * zn, width)
        for i in range(1, xn):
            send_xb(i).start()

    def end_x():
        total = xb_s[x]
        for i in range(1, xn):
            send_xb(i).wait_recv()
            total = total + xb[i]
        for zz in range(zn):
            for q in range(quarter):
                za_s[zz, 2 * q:2 * q + 2, :] = total[2 * zz:2 * zz + 2, q * lanes:(q + 1) * lanes]
        loop(1, zn, lambda i: send_za(i).start())

    def self_part():
        gout[...] = dot(tab[0:verts, :], grad_mean) + dot_b(grad_pre, ws[...])

    jobs = [self_part, start_y] + [functools.partial(step_y, k) for k in range(half_y - 1, -1, -1)] + [start_x, end_x]
    per_step = -(-len(jobs) // half_z)
    start_z()
    for hop in range(half_z - 1, -1, -1):
        for job in jobs[:per_step]:
            job()
        jobs = jobs[per_step:]
        if hop > 0:
            step_z(hop)
    for job in jobs:
        job()
    gout[...] += owed(0)
    for way, part in ((1, 1), (-1, 0), (1, 0), (-1, 1)):
        if goes(way, 1, part):
            rows = slice(part * cut, (part + 1) * cut)
            send_g(way, 1, part).wait_recv()
            gout[rows, :] += zin[(way + 1) // 2, 1, rows].astype(F32)
    loop(1, zn, lambda i: send_za(i).wait_recv())
    hub_sum = za_s[z]
    for i in range(1, zn):
        hub_sum = hub_sum + za[i]
    rows_of = lax.broadcasted_iota(jnp.int32, (verts, lanes), 0)
    for q in range(quarter):
        cols = slice(q * lanes, (q + 1) * lanes)
        gout[:, cols] += jnp.where(rows_of == hub0, hub_sum[2 * q:2 * q + 1], 0.0) + jnp.where(
            rows_of == hub1, hub_sum[2 * q + 1:2 * q + 2], 0.0
        )

    for hop in range(1, half_z + 1):
        for way, part in ((1, 0), (1, 1), (-1, 0), (-1, 1)):
            if goes(way, hop, part):
                send_z(way, hop, part).wait_send()
                send_g(way, hop, part).wait_send()
    for hop in range(1, half_y + 1):
        for way in (1, -1):
            send_y(way, hop).wait_send()
            send_h(way, hop).wait_send()
    for i in range(yn):
        send_sibg(i).wait_send()
    if xn > 1:
        for j in range(zn):
            given(j).wait_send()
    for i in range(1, xn):
        send_xb(i).wait_send()
    loop(1, zn, lambda i: send_za(i).wait_send())


def body(features, cotangent, w_self, w_neigh, bias, neighbours, send_rows, hub_local):
    verts, width = features.shape
    peers, slots = send_rows.shape[1:]
    xn, zn = peers // ZN, ZN
    groups = lax.axis_size("group")
    yn = groups // 2
    half_y, half_z = yn // 2, zn // 2
    near = peers * slots
    tall = xn * slots
    block = 2 * peers
    tile = width // 64
    lst = send_rows.reshape(xn, zn, slots).transpose(1, 0, 2).reshape(zn, tall).astype(F32)
    vmem = pl.BlockSpec(memory_space=pltpu.VMEM)
    dma = pltpu.SemaphoreType.DMA
    edge = (zn, xn, slots, width)
    ring = (half_y + 1, block, width)
    return pl.pallas_call(
        functools.partial(kernel, yn, xn, zn),
        out_shape=(
            jax.ShapeDtypeStruct((verts, width), BF16),
            jax.ShapeDtypeStruct((verts, width), F32),
        ),
        in_specs=[vmem] * 7 + [pl.BlockSpec(memory_space=pltpu.SMEM)],
        out_specs=(vmem, vmem),
        scratch_shapes=[
            pltpu.VMEM((verts + near + groups * block, verts), BF16),
            pltpu.VMEM((zn, verts, tall), BF16),
            pltpu.VMEM((zn, verts, width), BF16),
            pltpu.VMEM(edge, BF16),
            pltpu.VMEM(edge, BF16),
            pltpu.VMEM(edge, BF16),
            pltpu.VMEM(edge, BF16),
            pltpu.VMEM((2, half_z + 1, verts, width), BF16),
            pltpu.VMEM((2, half_z + 1, verts, width), BF16),
            pltpu.VMEM((groups, block, width), BF16),
            pltpu.VMEM((zn, tile + 8, 128), F32),
            pltpu.VMEM((zn, tile + 8, 128), F32),
            pltpu.VMEM((2 * zn, width), F32),
            pltpu.VMEM((xn, 2 * zn, width), F32),
            pltpu.VMEM((groups, block, width), F32),
            pltpu.VMEM((yn, block, width), F32),
            pltpu.VMEM(ring, F32),
            pltpu.VMEM(ring, F32),
            pltpu.VMEM(ring, F32),
            pltpu.VMEM(ring, F32),
            pltpu.VMEM((xn, 2 * zn, width), F32),
            pltpu.VMEM((xn, 2 * zn, width), F32),
            pltpu.VMEM((zn, tile, 128), F32),
            pltpu.VMEM((zn, tile, 128), F32),
            dma((2, 3, half_z + 1, 2)),
            dma((2, 3, half_z + 1, 2)),
            dma((2, 1)),
            dma((2, zn)),
            dma((2, zn)),
            dma((2, xn)),
            dma((2, 3, half_y + 1)),
            dma((2, yn)),
            dma((2, yn)),
            dma((2, 3, half_y + 1)),
            dma((2, xn)),
            dma((2, zn)),
        ],
        compiler_params=pltpu.CompilerParams(
            collective_id=0, has_side_effects=True, vmem_limit_bytes=60 * 1024 * 1024
        ),
    )(features, cotangent, w_self, w_neigh, bias.reshape(1, width), neighbours.T, lst, hub_local)


def solution(mesh):
    rows = P(("group", "dom"), None)
    return jax.shard_map(
        body,
        mesh=mesh,
        in_specs=(rows, rows, P(), P(), P(), rows, P(("group", "dom"), None, None), P(("group", "dom"))),
        out_specs=(rows, rows),
        check_vma=False,
    )
```

time: 142 us -> 126 us (0.89)
  Pallas kernels: 136 us -> 120 us
    pallas_call x1, Pallas kernels: 136 us -> 120 us  [body(): pl.pallas_call(functools.partial(kernel, yn, xn, zn), out_shape=(jax.Shap...]
    unnamed x5 -> x4, local copies, waits for them, and re-layouts: 3.32 us -> 2.52 us
where the time goes in v2:
time: 126 us; the launch traced here: 124 us
  Pallas kernels  120 us (95%)
  local copies, waits for them, and re-layouts  3.3 us (3%)
    pallas_call x1, Pallas kernels, body(): pl.pallas_call(functools.partial(kernel, yn, xn, zn), out_shape=(jax.Shap...  120 us
    unnamed x4, local copies, waits for them, and re-layouts  2.52 us

profile of v2, /device:TPU:6, one launch (start us, length us, event | category | flops | bytes accessed | tf_op | source)
XLA Modules:
  0.0 124.4 jit_solution(11931441040740106751)
XLA Ops:
  0.6 0.7 convert_element_type.9
  1.4 0.1 copy.11
  1.5 0.7 convert_element_type.12.lst
  2.1 119.7 %shard_map.95 = (bf16[256,512]{1,0:T(8,128)(2,1)}, f32[256,512]{1,0:T(8,128)}) custom-call(bf16[256,512]{1,0:T(8,128)(2,1)} %feat.1, bf16[256,512]{1,0:T(8,128)(2,1)} %cot.1, bf16[512,512]{1,0:T(8,128)(2,1)} %ws.1, bf16[512,512]{1,0:T(8,128)(2,1)} %wn.1, f32[1,512]{1,0:T(1,128)} %bitcast.5, s32[10,256]{1,0:T(8,128)} %bitcast.4, ...), custom_call_target="tpu_custom_call" | custom-call | tf_op jit(solution)/shard_map/pallas_call | solution.py:419
  121.8 0.0 copy-start
  121.8 1.7 %copy.15 = bf16[256,512]{1,0:T(8,128)(2,1)} copy(bf16[256,512]{1,0:T(8,128)(2,1)} %get-tuple-element.4) | data formatting | bytes 524288
  123.6 0.0 copy-done
  123.6 0.8 copy.16
  (2 shorter events, 0.0 us)
Async XLA Ops:
  121.8 1.7 %copy-start = (f32[256,512]{1,0:T(8,128)S(1)}, f32[256,512]{1,0:T(8,128)}, u32[]{:S(2)}) copy-start(f32[256,512]{1,0:T(8,128)} %get-tuple-element.5) | copy-start | bytes 1572868

commit v3 on v2

v3 whole, which is shorter than its diff:
```python
import functools

import jax
import jax.numpy as jnp
from jax import lax
from jax.experimental import pallas as pl
from jax.experimental.pallas import tpu as pltpu
from jax.sharding import PartitionSpec as P

ZN = 12
PARTS = 2
F32 = jnp.float32
BF16 = jnp.bfloat16


def dot_t(left, right):
    return lax.dot_general(left, right, (((0,), (0,)), ((), ())), preferred_element_type=F32)


def dot_b(left, right):
    return lax.dot_general(left, right, (((1,), (1,)), ((), ())), preferred_element_type=F32)


def dot(left, right):
    return jnp.dot(left, right, preferred_element_type=F32)


def kernel(
    yn, xn, zn, feat, cot, ws, wn, bias, nbrt, lst, hubl, out, gout,
    tab, sel, sel_b, rel, lists, zrows, xsend, bsend, arr, gsend, gback, gback_b, zout, zin, hubtab,
    ha_s, ha, hb_s, hb, hubg, sib_s, sib, yg_s, yg, xb_s, xb, za_s, za,
    sem_z, sem_rz, sem_l, sem_x, sem_b, sem_xg, sem_gb, sem_ha, sem_hb, sem_y, sem_sib, sem_sibg, sem_yg, sem_xb, sem_za,
):
    verts, width = feat.shape
    fanout = nbrt.shape[0]
    slots = arr.shape[2]
    lanes = 128
    tall = xn * slots
    quarter = width // lanes
    near = zn * tall
    hub_at = verts + near
    group = lax.axis_index("group")
    dom = lax.axis_index("dom")
    y, core = group // 2, lax.rem(group, 2)
    x, z = dom // zn, lax.rem(dom, zn)
    half_z = zn // 2
    hops = half_z - 2
    parts = sem_z.shape[3]
    cut = verts // parts

    def up_y(step):
        return lax.rem(y + step + 2 * yn, yn)

    def up_z(step):
        return lax.rem(z + step + 2 * zn, zn)

    def copy(src, dst, sems, at, **to):
        return pltpu.make_async_remote_copy(
            src_ref=src, dst_ref=dst, send_sem=sems.at[(0,) + at], recv_sem=sems.at[(1,) + at],
            device_id=to, device_id_type=pl.DeviceIdType.MESH,
        )

    def loop(lo, hi, body):
        lax.fori_loop(lo, hi, lambda i, c: (body(i), c)[1], 0)

    z_next = {1: {"dom": x * zn + up_z(1)}, -1: {"dom": x * zn + up_z(-1)}}
    sibling = {"group": y * 2 + 1 - core}

    barrier = pltpu.get_barrier_semaphore()

    def greet(**to):
        pl.semaphore_signal(barrier, 1, device_id=to, device_id_type=pl.DeviceIdType.MESH)

    loop(1, zn, lambda i: greet(dom=x * zn + up_z(i)))
    for i in range(1, xn):
        greet(dom=lax.rem(x + i, xn) * zn + z)
        for step in (-2, -1, 1, 2):
            greet(dom=lax.rem(x + i, xn) * zn + up_z(step))
    for i in range(1, yn):
        greet(group=up_y(i) * 2 + core)
    greet(**sibling)

    row_id = lax.broadcasted_iota(jnp.int32, (16, verts), 0)
    vert_id = lax.broadcasted_iota(jnp.int32, (16, verts), 1)
    hub0, hub1 = hubl[0], hubl[1]
    wanted = jnp.where(row_id == 0, hub0, jnp.where(row_id == 1, hub1, -1))
    hub_rows = dot((vert_id == wanted).astype(BF16), feat[...])
    for q in range(quarter):
        ha_s[2 * q:2 * q + 2, :] = hub_rows[0:2, q * lanes:(q + 1) * lanes]
    ha[z] = ha_s[...]
    rel[...] = jnp.full_like(rel, -1.0)
    for d in range(zn):
        rel[d:d + 1, :] = lst[pl.ds(up_z(d), 1), :]
    lists[z] = rel[...].astype(BF16)

    def tally(i):
        sub = lax.broadcasted_iota(jnp.int32, (tall, verts), 0)
        at = i * tall
        zz = i - verts // tall
        border = verts + zz * slots + (sub // slots) * (zn * slots) + lax.rem(sub, slots)
        is_border = jnp.logical_and(zz >= 0, zz < zn)
        rows = jnp.where(is_border, border, at + sub)
        total = jnp.zeros((tall, verts), F32)
        for e in range(fanout):
            total = jnp.where(nbrt[e:e + 1, :] == rows, total + 1.0, total)
        tab[pl.ds(pl.multiple_of(at, tall), tall), :] = total.astype(BF16)

    tiles = tab.shape[0] // tall
    spots = 2 * hops + 1
    cuts = [tiles * k // spots for k in range(spots + 1)]

    def tally_part(k):
        loop(cuts[k], cuts[k + 1], tally)

    tally_part(0)
    pl.semaphore_wait(barrier, zn - 1 + 5 * (xn - 1) + yn)

    def send_z(way, hop, part):
        owner = up_z(way * (1 - hop))
        rows = pl.ds(part * cut, cut)
        src = feat if hop == 1 else zrows.at[owner]
        return copy(src.at[rows], zrows.at[owner, rows], sem_z, (way + 1, hop, part), **z_next[way])

    def turns(first):
        for t in range(parts):
            part = (t + first) % parts
            yield 1, part
            yield -1, parts - 1 - part

    def send_ha(i):
        to = up_z(i)
        return copy(ha_s, ha.at[z], sem_ha, (i,), dom=x * zn + to)

    def send_l(way, hop):
        owner = lists.at[up_z(way * (1 - hop))]
        return copy(owner, owner, sem_l, (way + 1, hop), **z_next[way])

    loop(1, zn, lambda i: send_ha(i).start())
    send_l(1, 1).start()
    send_l(-1, 1).start()
    for way, part in turns(0):
        send_z(way, 1, part).start()

    sub_id = lax.broadcasted_iota(jnp.int32, (verts, tall), 0).astype(F32)

    def chosen_rows(owner, d, rows, sel_at, to_at):
        chosen = (sub_id == lists[owner, d % zn:d % zn + 1, :].astype(F32)).astype(BF16)
        sel_at[...] = chosen
        to_at[...] = dot_t(chosen, rows).astype(BF16).reshape(xn, slots, width)

    def pick(j):
        zz = up_z(j)
        chosen_rows(zz, -j, feat[...] if j == 0 else zrows[zz], sel.at[zz], xsend.at[zz])
        arr[zz, x] = xsend[zz, x]
        for i in range(1, xn):
            to = lax.rem(x + i, xn)
            copy(xsend.at[zz, to], arr.at[zz, x], sem_x, (0,), dom=to * zn + z).start()

    def far_of(way):
        return range(xn // 2) if way > 0 else range(xn // 2, xn)

    def b_slot(way, step):
        return (way + 1) // 2 if step == 1 else 2

    def pick_beyond(way, step):
        side, slot = (way + 1) // 2, b_slot(way, step)
        owner = up_z(-way * hops)
        rows = bsend.at[side, step - 1]
        chosen_rows(owner, way * (hops + step), zrows[owner], sel_b.at[side, step - 1], rows)
        for to in range(xn) if step == 1 else far_of(way):
            pltpu.make_async_remote_copy(
                src_ref=rows.at[to], dst_ref=arr.at[owner, x], send_sem=sem_b.at[0, slot, to], recv_sem=sem_b.at[1, slot, x],
                device_id={"dom": to * zn + up_z(way * step)}, device_id_type=pl.DeviceIdType.MESH,
            ).start()

    def hub_z():
        loop(1, zn, lambda i: send_ha(i).wait())
        for zz in range(zn):
            for q in range(quarter):
                hb_s[2 * zz:2 * zz + 2, q * lanes:(q + 1) * lanes] = ha[zz, 2 * q:2 * q + 2, :]
        hb[x] = hb_s[...]
        for i in range(1, xn):
            send_hb(i).start()

    def send_hb(i):
        return copy(hb_s, hb.at[x], sem_hb, (i,), dom=lax.rem(x + i, xn) * zn + z)

    block = hubtab.shape[1]

    def send_y(i):
        mine = hubtab.at[group]
        return copy(mine, mine, sem_y, (i,), group=up_y(i) * 2 + core)

    def send_sib(i):
        part = hubtab.at[up_y(-i) * 2 + core]
        return copy(part, part, sem_sib, (i,), **sibling)

    y_order = sorted(range(1, yn), key=lambda i: min(i, yn - i))

    def hub_x():
        for i in range(1, xn):
            send_hb(i).wait()
        hubtab[group] = hb[...].reshape(block, width).astype(BF16)
        for i in y_order:
            send_y(i).start()
        send_sib(0).start()

    def hub_y(some):
        for i in some:
            send_y(i).wait_recv()
            send_sib(i).start()

    near_y = (len(y_order) + 1) // 2
    last = 2 * hops - 1
    hub_steps = [
        (min(1, last), hub_z), (min(3, last), hub_x), (last, lambda: hub_y(y_order[:near_y])),
    ]
    spot = 0
    for hop in range(1, hops + 1):
        for t, (way, part) in enumerate(turns(0)):
            if t < 2:
                send_l(way, hop).wait_recv()
                if hop < hops:
                    send_l(way, hop + 1).start()
            send_z(way, hop, part).wait_recv()
            if hop < hops:
                send_z(way, hop + 1, part).start()
            if t == parts - 1:
                pick(1 - hop)
            elif t == 2 * parts - 1 and hop > 1:
                pick(hop - 1)
            if t % parts == parts - 1 and spot < last:
                for at, step in hub_steps:
                    if at == spot:
                        step()
                spot += 1
                tally_part(spot)
    for step in (2, 1):
        for way in (1, -1):
            pick_beyond(way, step)
    pick(-hops)
    pick(hops)
    for at, step in hub_steps:
        if at == spot:
            step()
    tally_part(spot + 1)
    hub_y(y_order[near_y:])

    agg = dot_t(tab[0:verts, :], feat[...])
    pre = dot(feat[...], ws[...]) + bias[...]
    for i in range(yn):
        send_sib(i).wait()
    agg += dot_t(tab[hub_at:, :], hubtab[...].reshape(2 * yn * block, width))
    if xn > 1:
        most = (pl.ds(0, 2 * hops + 1), pl.ds(0, xn - 1))
        copy(xsend.at[most], arr.at[most], sem_x, (0,), dom=lax.rem(x + 1, xn) * zn + z).wait()
    for slot in range(3):
        for i in range(xn):
            copy(bsend.at[0, 0, 0], arr.at[0, i], sem_b, (slot, i), **sibling).wait()
    agg += dot_t(tab[verts:hub_at, :], arr[...].reshape(near, width))

    mean = (agg / fanout).astype(BF16)
    pre += dot(mean, wn[...])
    sigm = jax.nn.sigmoid(pre)
    out[...] = (pre * sigm).astype(BF16)
    grad_pre = (cot[...].astype(F32) * sigm * (1.0 + pre * (1.0 - sigm))).astype(BF16)
    grad_mean = (dot_b(grad_pre, wn[...]) / fanout).astype(BF16)

    def slot_grads(zz):
        rows = pl.ds(pl.multiple_of(verts + zz * tall, tall), tall)
        gsend[zz] = dot(tab[rows, :], grad_mean).astype(BF16).reshape(xn, slots, width)

    def give_beyond(side, step, slot, to):
        way = 2 * side - 1
        return pltpu.make_async_remote_copy(
            src_ref=gsend.at[up_z(-way * (hops + step)), to], dst_ref=gback_b.at[side, step - 1, x],
            send_sem=sem_gb.at[0, slot, to], recv_sem=sem_gb.at[1, slot, x],
            device_id={"dom": to * zn + up_z(-way * step)}, device_id_type=pl.DeviceIdType.MESH,
        )

    my_side = 1 - x // (xn // 2)
    beyond = [(my_side, 2, 2), (1, 1, 1), (0, 1, 0)]
    for side, step, slot in beyond:
        slot_grads(up_z((1 - 2 * side) * (hops + step)))
        for to in range(xn):
            give_beyond(side, step, slot, to).start()
    gback_b[1, 1, xn // 2:] = jnp.zeros((xn // 2, slots, width), BF16)
    gback_b[0, 1, :xn // 2] = jnp.zeros((xn // 2, slots, width), BF16)

    def send_sibg(owner):
        return copy(sib_s.at[owner], sib.at[owner], sem_sibg, (owner,), **sibling)

    def hub_terms(owner):
        rows = pl.ds(pl.multiple_of(hub_at + owner * 2 * block, 32), 2 * block)
        hubg[pl.ds(2 * owner, 2)] = dot(tab[rows, :], grad_mean).reshape(2, block, width)
        sib_s[owner] = hubg[2 * owner + 1 - core].astype(BF16)
        send_sibg(owner).start()

    loop(0, yn, hub_terms)

    def give(t):
        j = lax.rem(jnp.where(lax.rem(t, 2) == 1, half_z - (t + 1) // 2, t // 2 - half_z) + zn, zn)
        zz = up_z(j)
        slot_grads(zz)
        gback[zz, x] = gsend[zz, x]
        for i in range(1, xn):
            to = lax.rem(x + i, xn)
            copy(gsend.at[zz, to], gback.at[zz, x], sem_xg, (j,), dom=to * zn + z).start()

    loop(3, zn, give)

    def given(j):
        some = pl.ds(0, xn - 1)
        zz = up_z(j)
        return copy(gsend.at[zz, some], gback.at[zz, some], sem_xg, (j % zn,), dom=lax.rem(x + 1, xn) * zn + z)

    def owed(j):
        if xn > 1:
            given(j).wait_recv()
        zz = up_z(j)
        value = dot(sel[zz], gback[zz].reshape(tall, width))
        if abs(j) == hops:
            way = 1 if j < 0 else -1
            side = (way + 1) // 2
            for step in (1, 2):
                slot = b_slot(way, step)
                for i in range(xn) if step == 1 else far_of(way):
                    copy(gsend.at[0, 0], gback_b.at[side, step - 1, i], sem_gb, (slot, i), **sibling).wait_recv()
                value += dot(sel_b[side, step - 1], gback_b[side, step - 1].reshape(tall, width))
        return value

    def send_g(way, hop, part):
        at, rows = (way + 1) // 2, pl.ds(part * cut, cut)
        return copy(zout.at[at, hop, rows], zin.at[at, hop, rows], sem_rz, (way + 1, hop, part), **z_next[way])

    def step_z(hop):
        terms = {1: owed(hop), -1: owed(-hop)}
        for way, part in turns(0):
            rows = slice(part * cut, (part + 1) * cut)
            value = terms[way][rows]
            if hop < hops:
                send_g(way, hop + 1, part).wait_recv()
                value = value + zin[(way + 1) // 2, hop + 1, rows].astype(F32)
            zout[(way + 1) // 2, hop, rows] = value.astype(BF16)
            send_g(way, hop, part).start()

    def mine(owner):
        return hubg[owner * 2 + core] + sib[owner].astype(F32)

    def send_yg(i):
        return copy(yg_s.at[i], yg.at[i], sem_yg, (i,), group=up_y(i) * 2 + core)

    def start_y():
        loop(0, yn, lambda i: send_sibg(i).wait_recv())

        def give_y(i):
            yg_s[i] = mine(up_y(i)).astype(BF16)
            send_yg(i).start()

        loop(1, yn, give_y)

    def send_xb(i):
        to = lax.rem(x + i, xn)
        return copy(xb_s.at[to], xb.at[i], sem_xb, (i,), dom=to * zn + z)

    def send_za(i):
        to = up_z(i)
        return copy(za_s.at[to], za.at[i], sem_za, (i,), dom=x * zn + to)

    def start_x():
        total = mine(y)
        for i in range(1, yn):
            send_yg(i).wait_recv()
            total = total + yg[i].astype(F32)
        xb_s[...] = total.reshape(xn, 2 * zn, width)
        for i in range(1, xn):
            send_xb(i).start()

    def end_x():
        total = xb_s[x]
        for i in range(1, xn):
            send_xb(i).wait_recv()
            total = total + xb[i]
        for zz in range(zn):
            for q in range(quarter):
                za_s[zz, 2 * q:2 * q + 2, :] = total[2 * zz:2 * zz + 2, q * lanes:(q + 1) * lanes]
        loop(1, zn, lambda i: send_za(i).start())

    def self_part():
        gout[...] = dot(tab[0:verts, :], grad_mean) + dot_b(grad_pre, ws[...])

    jobs = [(hops, self_part), (min(2, hops), start_x), (1, end_x)]
    start_y()
    for hop in range(hops, 0, -1):
        step_z(hop)
        for at, job in jobs:
            if at == hop:
                job()
    gout[...] += owed(0)
    for way, part in turns(0):
        rows = slice(part * cut, (part + 1) * cut)
        send_g(way, 1, part).wait_recv()
        gout[rows, :] += zin[(way + 1) // 2, 1, rows].astype(F32)
    loop(1, zn, lambda i: send_za(i).wait_recv())
    hub_sum = za_s[z]
    for i in range(1, zn):
        hub_sum = hub_sum + za[i]
    rows_of = lax.broadcasted_iota(jnp.int32, (verts, lanes), 0)
    for q in range(quarter):
        cols = slice(q * lanes, (q + 1) * lanes)
        gout[:, cols] += jnp.where(rows_of == hub0, hub_sum[2 * q:2 * q + 1], 0.0) + jnp.where(
            rows_of == hub1, hub_sum[2 * q + 1:2 * q + 2], 0.0
        )

    for hop in range(1, hops + 1):
        for way, part in turns(0):
            send_z(way, hop, part).wait_send()
            send_g(way, hop, part).wait_send()
        send_l(1, hop).wait_send()
        send_l(-1, hop).wait_send()
    for i in range(1, yn):
        send_y(i).wait_send()
        send_yg(i).wait_send()
    for i in range(yn):
        send_sibg(i).wait_send()
    if xn > 1:
        for j in range(zn):
            if min(j, zn - j) <= hops:
                given(j).wait_send()
    for side, step, slot in beyond:
        for to in range(xn):
            give_beyond(side, step, slot, to).wait_send()
    for i in range(1, xn):
        send_xb(i).wait_send()
    loop(1, zn, lambda i: send_za(i).wait_send())


def body(features, cotangent, w_self, w_neigh, bias, neighbours, send_rows, hub_local):
    verts, width = features.shape
    peers, slots = send_rows.shape[1:]
    xn, zn = peers // ZN, ZN
    groups = lax.axis_size("group")
    yn = groups // 2
    half_z, parts = zn // 2, PARTS
    near = peers * slots
    tall = xn * slots
    block = 2 * peers
    tile = width // 64
    lst = send_rows.reshape(xn, zn, slots).transpose(1, 0, 2).reshape(zn, tall).astype(F32)
    vmem = pl.BlockSpec(memory_space=pltpu.VMEM)
    dma = pltpu.SemaphoreType.DMA
    edge = (zn, xn, slots, width)
    hub = (yn, block, width)
    return pl.pallas_call(
        functools.partial(kernel, yn, xn, zn),
        out_shape=(
            jax.ShapeDtypeStruct((verts, width), BF16),
            jax.ShapeDtypeStruct((verts, width), F32),
        ),
        in_specs=[vmem] * 7 + [pl.BlockSpec(memory_space=pltpu.SMEM)],
        out_specs=(vmem, vmem),
        scratch_shapes=[
            pltpu.VMEM((verts + near + groups * block, verts), BF16),
            pltpu.VMEM((zn, verts, tall), BF16),
            pltpu.VMEM((2, 2, verts, tall), BF16),
            pltpu.VMEM((16, tall), F32),
            pltpu.VMEM((zn, 16, tall), BF16),
            pltpu.VMEM((zn, verts, width), BF16),
            pltpu.VMEM(edge, BF16),
            pltpu.VMEM((2, 2) + edge[1:], BF16),
            pltpu.VMEM(edge, BF16),
            pltpu.VMEM(edge, BF16),
            pltpu.VMEM(edge, BF16),
            pltpu.VMEM((2, 2) + edge[1:], BF16),
            pltpu.VMEM((2, half_z - 1, verts, width), BF16),
            pltpu.VMEM((2, half_z - 1, verts, width), BF16),
            pltpu.VMEM((groups, block, width), BF16),
            pltpu.VMEM((tile, 128), F32),
            pltpu.VMEM((zn, tile, 128), F32),
            pltpu.VMEM((2 * zn, width), F32),
            pltpu.VMEM((xn, 2 * zn, width), F32),
            pltpu.VMEM((groups, block, width), F32),
            pltpu.VMEM(hub, BF16),
            pltpu.VMEM(hub, BF16),
            pltpu.VMEM(hub, BF16),
            pltpu.VMEM(hub, BF16),
            pltpu.VMEM((xn, 2 * zn, width), F32),
            pltpu.VMEM((xn, 2 * zn, width), F32),
            pltpu.VMEM((zn, tile, 128), F32),
            pltpu.VMEM((zn, tile, 128), F32),
            dma((2, 3, half_z, parts)),
            dma((2, 3, half_z, parts)),
            dma((2, 3, half_z)),
            dma((2, 1)),
            dma((2, 3, xn)),
            dma((2, zn)),
            dma((2, 3, xn)),
            dma((2, zn)),
            dma((2, xn)),
            dma((2, yn)),
            dma((2, yn)),
            dma((2, yn)),
            dma((2, yn)),
            dma((2, xn)),
            dma((2, zn)),
        ],
        compiler_params=pltpu.CompilerParams(
            collective_id=0, has_side_effects=True, vmem_limit_bytes=60 * 1024 * 1024
        ),
    )(features, cotangent, w_self, w_neigh, bias.reshape(1, width), neighbours.T, lst, hub_local)


def solution(mesh):
    rows = P(("group", "dom"), None)
    return jax.shard_map(
        body,
        mesh=mesh,
        in_specs=(rows, rows, P(), P(), P(), rows, P(("group", "dom"), None, None), P(("group", "dom"))),
        out_specs=(rows, rows),
        check_vma=False,
    )
```

time: 126 us -> 108 us (0.86)
  Pallas kernels: 120 us -> 103 us
    pallas_call x1, Pallas kernels: 120 us -> 103 us  [body(): pl.pallas_call(functools.partial(kernel, yn, xn, zn), out_shape=(jax.Shap...]
where the time goes in v3:
time: 108 us; the launch traced here: 107 us
  Pallas kernels  103 us (95%)
  local copies, waits for them, and re-layouts  3.3 us (3%)
    pallas_call x1, Pallas kernels, body(): pl.pallas_call(functools.partial(kernel, yn, xn, zn), out_shape=(jax.Shap...  103 us
    unnamed x4, local copies, waits for them, and re-layouts  2.52 us

profile of v3, /device:TPU:6, one launch (start us, length us, event | category | flops | bytes accessed | tf_op | source)
XLA Modules:
  0.0 107.3 jit_solution(8555915733070444337)
XLA Ops:
  0.6 0.7 convert_element_type.9
  1.4 0.1 copy.11
  1.5 0.7 convert_element_type.12.lst
  2.1 102.7 %shard_map.95 = (bf16[256,512]{1,0:T(8,128)(2,1)}, f32[256,512]{1,0:T(8,128)}) custom-call(bf16[256,512]{1,0:T(8,128)(2,1)} %feat.1, bf16[256,512]{1,0:T(8,128)(2,1)} %cot.1, bf16[512,512]{1,0:T(8,128)(2,1)} %ws.1, bf16[512,512]{1,0:T(8,128)(2,1)} %wn.1, f32[1,512]{1,0:T(1,128)} %bitcast.5, s32[10,256]{1,0:T(8,128)} %bitcast.4, ...), custom_call_target="tpu_custom_call" | custom-call | tf_op jit(solution)/shard_map/pallas_call | solution.py:454
  104.8 0.0 copy-start
  104.8 1.7 %copy.15 = bf16[256,512]{1,0:T(8,128)(2,1)} copy(bf16[256,512]{1,0:T(8,128)(2,1)} %get-tuple-element.4) | data formatting | bytes 524288
  106.6 0.0 copy-done
  106.6 0.8 copy.16
  (2 shorter events, 0.0 us)
Async XLA Ops:
  104.8 1.7 %copy-start = (f32[256,512]{1,0:T(8,128)S(1)}, f32[256,512]{1,0:T(8,128)}, u32[]{:S(2)}) copy-start(f32[256,512]{1,0:T(8,128)} %get-tuple-element.5) | copy-start | bytes 1572868

commit v4 on v3

v4 whole, which is shorter than its diff:
```python
import functools

import jax
import jax.numpy as jnp
from jax import lax
from jax.experimental import pallas as pl
from jax.experimental.pallas import tpu as pltpu
from jax.sharding import PartitionSpec as P

ZN = 12
PARTS = 2
F32 = jnp.float32
BF16 = jnp.bfloat16


def dot_t(left, right):
    return lax.dot_general(left, right, (((0,), (0,)), ((), ())), preferred_element_type=F32)


def dot_b(left, right):
    return lax.dot_general(left, right, (((1,), (1,)), ((), ())), preferred_element_type=F32)


def dot(left, right):
    return jnp.dot(left, right, preferred_element_type=F32)


def kernel(
    yn, xn, zn, feat_in, cot_in, ws_in, wn_in, bias_in, nbrt_in, sr_in, hubl, out, gout,
    feat, cot, ws, wn, bias, nbrt, sr, lst, outv, gm,
    tab, sel, sel_b, rel, lists, zrows, xsend, bsend, arr, gsend, gback, gback_b, zout, zin, hubtab,
    ha_s, ha, hb_s, hb, hubg, sib_s, sib, yg_s, yg, xb_s, xb, za_s, za,
    sem_z, sem_rz, sem_l, sem_x, sem_b, sem_xg, sem_gb, sem_ha, sem_hb, sem_y, sem_sib, sem_sibg, sem_yg, sem_xb, sem_za, sem_in,
):
    verts, width = feat.shape
    fanout = nbrt.shape[0]
    slots = arr.shape[3]
    lanes = 128
    tall = xn * slots
    quarter = width // lanes
    near = zn * tall
    hub_at = verts + near
    group = lax.axis_index("group")
    dom = lax.axis_index("dom")
    y, core = group // 2, lax.rem(group, 2)
    x, z = dom // zn, lax.rem(dom, zn)
    half_z = zn // 2
    hops = half_z - 2
    parts = sem_z.shape[3]
    cut = width // parts

    def up_y(step):
        return lax.rem(y + step + 2 * yn, yn)

    def up_z(step):
        return lax.rem(z + step + 2 * zn, zn)

    def copy(src, dst, sems, at, **to):
        return pltpu.make_async_remote_copy(
            src_ref=src, dst_ref=dst, send_sem=sems.at[(0,) + at], recv_sem=sems.at[(1,) + at],
            device_id=to, device_id_type=pl.DeviceIdType.MESH,
        )

    def loop(lo, hi, body):
        lax.fori_loop(lo, hi, lambda i, c: (body(i), c)[1], 0)

    z_next = {1: {"dom": x * zn + up_z(1)}, -1: {"dom": x * zn + up_z(-1)}}
    sibling = {"group": y * 2 + 1 - core}

    barrier = pltpu.get_barrier_semaphore()

    def greet(**to):
        pl.semaphore_signal(barrier, 1, device_id=to, device_id_type=pl.DeviceIdType.MESH)

    loop(1, zn, lambda i: greet(dom=x * zn + up_z(i)))
    for i in range(1, xn):
        greet(dom=lax.rem(x + i, xn) * zn + z)
        for step in (-2, -1, 1, 2):
            greet(dom=lax.rem(x + i, xn) * zn + up_z(step))
    for step in (-2, -1, 1, 2):
        greet(group=up_y(step) * 2 + core)
    greet(**sibling)

    sources = (feat_in, sr_in, nbrt_in, cot_in, ws_in, wn_in, bias_in)
    loads = [
        pltpu.make_async_copy(src, dst, sem_in.at[i])
        for i, (src, dst) in enumerate(zip(sources, (feat, sr, nbrt, cot, ws, wn, bias)))
    ]
    for part in range(parts):
        cols = feat_in.at[:, pl.ds(part * cut, cut)]
        loads.append(pltpu.make_async_copy(cols, zrows.at[z, part], sem_in.at[7 + part]))
    for i in (0, 1, 7, 2, 3, 4, 5, 6):
        loads[i].start()
    for load in loads[8:]:
        load.start()
    loads[0].wait()

    row_id = lax.broadcasted_iota(jnp.int32, (16, verts), 0)
    vert_id = lax.broadcasted_iota(jnp.int32, (16, verts), 1)
    hub0, hub1 = hubl[0], hubl[1]
    wanted = jnp.where(row_id == 0, hub0, jnp.where(row_id == 1, hub1, -1))
    hub_rows = dot((vert_id == wanted).astype(BF16), feat[...])
    for q in range(quarter):
        ha_s[2 * q:2 * q + 2, :] = hub_rows[0:2, q * lanes:(q + 1) * lanes]
    ha[z] = ha_s[...]
    loads[1].wait()
    by_peer = sr[...].astype(F32).T
    for xx in range(xn):
        lst[:, xx * slots:(xx + 1) * slots] = by_peer[xx * zn:(xx + 1) * zn, :]
    rel[...] = jnp.full_like(rel, -1.0)
    for d in range(zn):
        rel[d:d + 1, :] = lst[pl.ds(up_z(d), 1), :]
    lists[z] = rel[...].astype(BF16)

    def tally(i):
        sub = lax.broadcasted_iota(jnp.int32, (tall, verts), 0)
        at = i * tall
        zz = i - verts // tall
        border = verts + zz * slots + (sub // slots) * (zn * slots) + lax.rem(sub, slots)
        is_border = jnp.logical_and(zz >= 0, zz < zn)
        rows = jnp.where(is_border, border, at + sub)
        total = jnp.zeros((tall, verts), F32)
        for e in range(fanout):
            total = jnp.where(nbrt[e:e + 1, :] == rows, total + 1.0, total)
        tab[pl.ds(pl.multiple_of(at, tall), tall), :] = total.astype(BF16)

    tiles = tab.shape[0] // tall
    spots = 2 * hops + 1
    cuts = [tiles * k // spots for k in range(spots + 1)]

    def tally_part(k):
        loop(cuts[k], cuts[k + 1], tally)

    loads[2].wait()
    tally_part(0)
    for load in loads[7:]:
        load.wait()
    pl.semaphore_wait(barrier, zn - 1 + 5 * (xn - 1) + 5)

    def send_z(way, hop, part):
        piece = zrows.at[up_z(way * (1 - hop)), part]
        return copy(piece, piece, sem_z, (way + 1, hop, part), **z_next[way])

    turns = [(way, part) for part in range(parts) for way in (1, -1)]

    def send_ha(i):
        to = up_z(i)
        return copy(ha_s, ha.at[z], sem_ha, (i,), dom=x * zn + to)

    def send_l(way, hop):
        owner = lists.at[up_z(way * (1 - hop))]
        return copy(owner, owner, sem_l, (way + 1, hop), **z_next[way])

    loop(1, zn, lambda i: send_ha(i).start())
    send_l(1, 1).start()
    send_l(-1, 1).start()
    for way, part in turns:
        send_z(way, 1, part).start()

    sub_id = lax.broadcasted_iota(jnp.int32, (verts, tall), 0).astype(F32)

    def chosen_rows(owner, d, part, sel_at, to_at):
        if part == 0:
            sel_at[...] = (sub_id == lists[owner, d % zn:d % zn + 1, :].astype(F32)).astype(BF16)
        to_at[...] = dot_t(sel_at[...], zrows[owner, part]).astype(BF16).reshape(xn, slots, cut)

    def pick(j, part):
        zz = up_z(j)
        chosen_rows(zz, -j, part, sel.at[zz], xsend.at[zz, part])
        arr[part, zz, x] = xsend[zz, part, x]
        for i in range(1, xn):
            to = lax.rem(x + i, xn)
            copy(xsend.at[zz, part, to], arr.at[part, zz, x], sem_x, (part,), dom=to * zn + z).start()

    def far_of(way):
        return range(xn // 2) if way > 0 else range(xn // 2, xn)

    def b_slot(way, step):
        return (way + 1) // 2 if step == 1 else 2

    def pick_beyond(way, step, part):
        side, slot = (way + 1) // 2, 3 * part + b_slot(way, step)
        owner = up_z(-way * hops)
        rows = bsend.at[side, step - 1, part]
        chosen_rows(owner, way * (hops + step), part, sel_b.at[side, step - 1], rows)
        for to in range(xn) if step == 1 else far_of(way):
            pltpu.make_async_remote_copy(
                src_ref=rows.at[to], dst_ref=arr.at[part, owner, x],
                send_sem=sem_b.at[0, slot, to], recv_sem=sem_b.at[1, slot, x],
                device_id={"dom": to * zn + up_z(way * step)}, device_id_type=pl.DeviceIdType.MESH,
            ).start()

    def hub_z():
        loop(1, zn, lambda i: send_ha(i).wait())
        for zz in range(zn):
            for q in range(quarter):
                hb_s[2 * zz:2 * zz + 2, q * lanes:(q + 1) * lanes] = ha[zz, 2 * q:2 * q + 2, :]
        hb[x] = hb_s[...]
        for i in range(1, xn):
            send_hb(i).start()

    def send_hb(i):
        return copy(hb_s, hb.at[x], sem_hb, (i,), dom=lax.rem(x + i, xn) * zn + z)

    block = hubtab.shape[1]

    lower, upper = pl.ds(0, block // 2), pl.ds(block // 2, block // 2)

    def y_peer(step):
        return {"group": up_y(step) * 2 + core}

    def send_y(i):
        if abs(i) in (1, 2):
            owner, to = y, i
        else:
            owner, to = (up_y(2), -(i == -3) or -2) if i <= 0 else (up_y(-2), i - 2)
        piece = hubtab.at[owner * 2 + core]
        if i in (0, 4):
            piece = piece.at[upper if i == 0 else lower]
        return copy(piece, piece, sem_y, (i % yn,), **y_peer(to))

    def send_sib(i):
        part = hubtab.at[up_y(-i) * 2 + core]
        return copy(part, part, sem_sib, (i,), **sibling)

    def hub_x():
        for i in range(1, xn):
            send_hb(i).wait()
        hubtab[group] = hb[...].reshape(block, width).astype(BF16)
        for i in (2, -2, 1, -1):
            send_y(i).start()
        send_sib(0).start()

    def hub_y():
        send_y(2).wait_recv()
        send_y(3).start()
        send_y(4).start()
        send_y(-2).wait_recv()
        send_y(-3).start()
        send_y(0).start()
        for i in (2, yn - 2):
            send_sib(i).start()
        for i in (1, -1):
            send_y(i).wait_recv()
            send_sib(i % yn).start()

    def hub_end():
        for i in (3, -3, 4):
            send_y(i).wait_recv()
            if i == 4:
                send_y(0).wait_recv()
            send_sib(i % yn).start()

    last = 2 * hops - 1
    hub_steps = [(min(1, last), hub_z), (min(3, last), hub_x), (max(last - 1, 1), hub_y)]
    for part in range(parts):
        pick(0, part)
    spot = 0
    for hop in range(1, hops + 1):
        for way in (1, -1):
            send_l(way, hop).wait_recv()
            if hop < hops:
                send_l(way, hop + 1).start()
        for part in range(parts):
            for way in (1, -1):
                send_z(way, hop, part).wait_recv()
                if hop < hops:
                    send_z(way, hop + 1, part).start()
                else:
                    pick_beyond(way, 1, part)
                    pick_beyond(way, 2, part)
            pick(-hop, part)
            pick(hop, part)
            if part in (parts // 2 - 1, parts - 1) and spot < last:
                for at, step in hub_steps:
                    if at == spot:
                        step()
                spot += 1
                tally_part(spot)
    for at, step in hub_steps:
        if at == spot:
            step()
    tally_part(spot + 1)
    hub_end()

    for load in loads[3:7]:
        load.wait()
    agg = dot_t(tab[0:verts, :], feat[...])
    pre = dot(feat[...], ws[...]) + bias[...]
    for i in range(yn):
        send_sib(i).wait()
    agg += dot_t(tab[hub_at:, :], hubtab[...].reshape(2 * yn * block, width))
    for part in range(parts):
        cols = slice(part * cut, (part + 1) * cut)
        if xn > 1:
            most = (pl.ds(0, 2 * hops + 1), pl.ds(0, xn - 1))
            whole = arr.at[part].at[most]
            copy(whole, whole, sem_x, (part,), dom=lax.rem(x + 1, xn) * zn + z).wait()
        for slot in range(3):
            for i in range(xn):
                copy(bsend.at[0, 0, part, 0], arr.at[part, 0, i], sem_b, (3 * part + slot, i), **sibling).wait()
        summed = agg[:, cols] + dot_t(tab[verts:hub_at, :], arr[part].reshape(near, cut))
        pre += dot((summed / fanout).astype(BF16), wn[cols, :])
    sigm = jax.nn.sigmoid(pre)
    outv[...] = (pre * sigm).astype(BF16)
    store = pltpu.make_async_copy(outv, out, sem_in.at[0])
    store.start()
    grad_pre = (cot[...].astype(F32) * sigm * (1.0 + pre * (1.0 - sigm))).astype(BF16)
    grad_mean = (dot_b(grad_pre, wn[...]) / fanout).astype(BF16)
    for part in range(parts):
        gm[part] = grad_mean[:, part * cut:(part + 1) * cut]

    def slot_grads(zz, part):
        rows = pl.ds(pl.multiple_of(verts + zz * tall, tall), tall)
        gsend[zz, part] = dot(tab[rows, :], gm[part]).astype(BF16).reshape(xn, slots, cut)

    def give_beyond(side, step, slot, to, part):
        way = 2 * side - 1
        return pltpu.make_async_remote_copy(
            src_ref=gsend.at[up_z(-way * (hops + step)), part, to], dst_ref=gback_b.at[side, step - 1, part, x],
            send_sem=sem_gb.at[0, 3 * part + slot, to], recv_sem=sem_gb.at[1, 3 * part + slot, x],
            device_id={"dom": to * zn + up_z(-way * step)}, device_id_type=pl.DeviceIdType.MESH,
        )

    my_side = 1 - x // (xn // 2)
    beyond = [(my_side, 2, 2), (1, 1, 1), (0, 1, 0)]

    def give(j, part):
        zz = up_z(j)
        slot_grads(zz, part)
        gback[zz, part, x] = gsend[zz, part, x]
        for i in range(1, xn):
            to = lax.rem(x + i, xn)
            copy(gsend.at[zz, part, to], gback.at[zz, part, x], sem_xg, (j * parts + part,), dom=to * zn + z).start()

    def give_first(part):
        for side, step, slot in beyond:
            slot_grads(up_z((1 - 2 * side) * (hops + step)), part)
            for to in range(xn):
                give_beyond(side, step, slot, to, part).start()
        give(hops, part)
        give(zn - hops, part)

    give_first(0)
    gback_b[1, 1, :, xn // 2:] = jnp.zeros((parts, xn // 2, slots, cut), BF16)
    gback_b[0, 1, :, :xn // 2] = jnp.zeros((parts, xn // 2, slots, cut), BF16)

    def send_sibg(owner):
        return copy(sib_s.at[owner], sib.at[owner], sem_sibg, (owner,), **sibling)

    def hub_terms(owner):
        rows = pl.ds(pl.multiple_of(hub_at + owner * 2 * block, 32), 2 * block)
        hubg[pl.ds(2 * owner, 2)] = dot(tab[rows, :], grad_mean).reshape(2, block, width)
        sib_s[owner] = hubg[2 * owner + 1 - core].astype(BF16)
        send_sibg(owner).start()

    loop(0, yn, hub_terms)

    for part in range(1, parts):
        give_first(part)

    def give_rest(t):
        j = lax.rem(jnp.where(lax.rem(t, 2) == 1, half_z - (t + 1) // 2, t // 2 - half_z) + zn, zn)
        for part in range(parts):
            give(j, part)

    loop(5, zn, give_rest)

    def given(j, part):
        some = pl.ds(0, xn - 1)
        zz = up_z(j)
        at = (j % zn) * parts + part
        return copy(gsend.at[zz, part, some], gback.at[zz, part, some], sem_xg, (at,), dom=lax.rem(x + 1, xn) * zn + z)

    def owed(j, part):
        if xn > 1:
            given(j, part).wait_recv()
        zz = up_z(j)
        value = dot(sel[zz], gback[zz, part].reshape(tall, cut))
        if abs(j) == hops:
            way = 1 if j < 0 else -1
            side = (way + 1) // 2
            for step in (1, 2):
                slot = 3 * part + b_slot(way, step)
                for i in range(xn) if step == 1 else far_of(way):
                    copy(gsend.at[0, part, 0], gback_b.at[side, step - 1, part, i], sem_gb, (slot, i), **sibling).wait_recv()
                value += dot(sel_b[side, step - 1], gback_b[side, step - 1, part].reshape(tall, cut))
        return value

    def send_g(way, hop, part):
        at = ((way + 1) // 2, hop, part)
        return copy(zout.at[at], zin.at[at], sem_rz, (way + 1, hop, part), **z_next[way])

    def step_z(hop):
        for way, part in turns:
            at = (way + 1) // 2
            value = owed(way * hop, part)
            if hop < hops:
                send_g(way, hop + 1, part).wait_recv()
                value = value + zin[at, hop + 1, part].astype(F32)
            zout[at, hop, part] = value.astype(BF16)
            send_g(way, hop, part).start()

    def mine(owner):
        return hubg[owner * 2 + core] + sib[owner].astype(F32)

    reach = (1, -1, 2, -2, 1, -1, 2, -2)

    def send_yg(i):
        src, dst = yg_s.at[i], yg.at[i]
        if i in (2, 3):
            rows = lower if i == 2 else upper
            src, dst = src.at[rows], dst.at[rows]
        return copy(src, dst, sem_yg, (i,), **y_peer(reach[i]))

    def start_y():
        loop(0, yn, lambda i: send_sibg(i).wait_recv())
        for i, owner in enumerate((3, -3, 4, -4, 1, -1)):
            yg_s[i] = mine(up_y(owner)).astype(BF16)
            send_yg(i).start()

    def relay_y():
        for i in (0, 1):
            send_yg(i).wait_recv()
            send_yg(i + 2).wait_recv()
            value = mine(up_y(reach[i + 6])) + yg[i].astype(F32)
            for at, some in ((0, slice(0, block // 2)), (1, slice(block // 2, block))):
                term = value[some]
                if at == i:
                    term = term + yg[i + 2, some].astype(F32)
                yg_s[i + 6, some] = term.astype(BF16)
            send_yg(i + 6).start()

    def send_xb(i):
        to = lax.rem(x + i, xn)
        return copy(xb_s.at[to], xb.at[i], sem_xb, (i,), dom=to * zn + z)

    def send_za(i):
        to = up_z(i)
        return copy(za_s.at[to], za.at[i], sem_za, (i,), dom=x * zn + to)

    def start_x():
        total = mine(y)
        for i in range(4, 8):
            send_yg(i).wait_recv()
            total = total + yg[i].astype(F32)
        xb_s[...] = total.reshape(xn, 2 * zn, width)
        for i in range(1, xn):
            send_xb(i).start()

    def end_x():
        total = xb_s[x]
        for i in range(1, xn):
            send_xb(i).wait_recv()
            total = total + xb[i]
        for zz in range(zn):
            for q in range(quarter):
                za_s[zz, 2 * q:2 * q + 2, :] = total[2 * zz:2 * zz + 2, q * lanes:(q + 1) * lanes]
        loop(1, zn, lambda i: send_za(i).start())

    def self_part():
        gout[...] = dot(tab[0:verts, :], grad_mean) + dot_b(grad_pre, ws[...])

    def wait_sent():
        for hop in range(1, hops + 1):
            for way, part in turns:
                send_z(way, hop, part).wait_send()
            send_l(1, hop).wait_send()
            send_l(-1, hop).wait_send()
        for i in (1, -1, 2, -2, 3, -3, 4, 0):
            send_y(i).wait_send()
        store.wait()

    def wait_given():
        for hop in range(2, hops + 1):
            for way, part in turns:
                send_g(way, hop, part).wait_send()
        for i in range(8):
            send_yg(i).wait_send()
        for i in range(yn):
            send_sibg(i).wait_send()
        for part in range(parts):
            if xn > 1:
                for j in range(zn):
                    if min(j, zn - j) <= hops:
                        given(j, part).wait_send()
            for side, step, slot in beyond:
                for to in range(xn):
                    give_beyond(side, step, slot, to, part).wait_send()

    jobs = [(hops, self_part), (hops, wait_sent), (hops, relay_y), (min(2, hops), start_x), (1, end_x), (1, wait_given)]
    start_y()
    for hop in range(hops, 0, -1):
        step_z(hop)
        for at, job in jobs:
            if at == hop:
                job()
    for part in range(parts):
        cols = slice(part * cut, (part + 1) * cut)
        gout[:, cols] += owed(0, part)
    for way, part in turns:
        cols = slice(part * cut, (part + 1) * cut)
        send_g(way, 1, part).wait_recv()
        gout[:, cols] += zin[(way + 1) // 2, 1, part].astype(F32)
    loop(1, zn, lambda i: send_za(i).wait_recv())
    hub_sum = za_s[z]
    for i in range(1, zn):
        hub_sum = hub_sum + za[i]
    rows_of = lax.broadcasted_iota(jnp.int32, (verts, lanes), 0)
    for q in range(quarter):
        cols = slice(q * lanes, (q + 1) * lanes)
        gout[:, cols] += jnp.where(rows_of == hub0, hub_sum[2 * q:2 * q + 1], 0.0) + jnp.where(
            rows_of == hub1, hub_sum[2 * q + 1:2 * q + 2], 0.0
        )

    for way, part in turns:
        send_g(way, 1, part).wait_send()
    for i in range(1, xn):
        send_xb(i).wait_send()
    loop(1, zn, lambda i: send_za(i).wait_send())


def body(features, cotangent, w_self, w_neigh, bias, neighbours, send_rows, hub_local):
    verts, width = features.shape
    peers, slots = send_rows.shape[1:]
    xn, zn = peers // ZN, ZN
    groups = lax.axis_size("group")
    yn = groups // 2
    half_z, parts = zn // 2, PARTS
    near = peers * slots
    tall = xn * slots
    block = 2 * peers
    tile = width // 64
    cut = width // parts
    vmem = pl.BlockSpec(memory_space=pltpu.VMEM)
    dma = pltpu.SemaphoreType.DMA
    edge = (zn, parts, xn, slots, cut)
    hub = (yn, block, width)
    return pl.pallas_call(
        functools.partial(kernel, yn, xn, zn),
        out_shape=(
            jax.ShapeDtypeStruct((verts, width), BF16),
            jax.ShapeDtypeStruct((verts, width), F32),
        ),
        in_specs=[pl.BlockSpec(memory_space=pl.ANY)] * 7 + [pl.BlockSpec(memory_space=pltpu.SMEM)],
        out_specs=(pl.BlockSpec(memory_space=pl.ANY), vmem),
        scratch_shapes=[
            pltpu.VMEM((verts, width), BF16),
            pltpu.VMEM((verts, width), BF16),
            pltpu.VMEM((width, width), BF16),
            pltpu.VMEM((width, width), BF16),
            pltpu.VMEM((1, width), F32),
            pltpu.VMEM(neighbours.shape[::-1], jnp.int32),
            pltpu.VMEM((slots, peers), jnp.int32),
            pltpu.VMEM((zn, tall), F32),
            pltpu.VMEM((verts, width), BF16),
            pltpu.VMEM((parts, verts, cut), BF16),
            pltpu.VMEM((verts + near + groups * block, verts), BF16),
            pltpu.VMEM((zn, verts, tall), BF16),
            pltpu.VMEM((2, 2, verts, tall), BF16),
            pltpu.VMEM((16, tall), F32),
            pltpu.VMEM((zn, 16, tall), BF16),
            pltpu.VMEM((zn, parts, verts, cut), BF16),
            pltpu.VMEM(edge, BF16),
            pltpu.VMEM((2, 2) + edge[1:], BF16),
            pltpu.VMEM((parts, zn, xn, slots, cut), BF16),
            pltpu.VMEM(edge, BF16),
            pltpu.VMEM(edge, BF16),
            pltpu.VMEM((2, 2) + edge[1:], BF16),
            pltpu.VMEM((2, half_z - 1, parts, verts, cut), BF16),
            pltpu.VMEM((2, half_z - 1, parts, verts, cut), BF16),
            pltpu.VMEM((groups, block, width), BF16),
            pltpu.VMEM((tile, 128), F32),
            pltpu.VMEM((zn, tile, 128), F32),
            pltpu.VMEM((2 * zn, width), F32),
            pltpu.VMEM((xn, 2 * zn, width), F32),
            pltpu.VMEM((groups, block, width), F32),
            pltpu.VMEM(hub, BF16),
            pltpu.VMEM(hub, BF16),
            pltpu.VMEM(hub, BF16),
            pltpu.VMEM(hub, BF16),
            pltpu.VMEM((xn, 2 * zn, width), F32),
            pltpu.VMEM((xn, 2 * zn, width), F32),
            pltpu.VMEM((zn, tile, 128), F32),
            pltpu.VMEM((zn, tile, 128), F32),
            dma((2, 3, half_z, parts)),
            dma((2, 3, half_z, parts)),
            dma((2, 3, half_z)),
            dma((2, parts)),
            dma((2, 3 * parts, xn)),
            dma((2, zn * parts)),
            dma((2, 3 * parts, xn)),
            dma((2, zn)),
            dma((2, xn)),
            dma((2, yn)),
            dma((2, yn)),
            dma((2, yn)),
            dma((2, yn)),
            dma((2, xn)),
            dma((2, zn)),
            dma((7 + parts,)),
        ],
        compiler_params=pltpu.CompilerParams(
            collective_id=0, has_side_effects=True, vmem_limit_bytes=60 * 1024 * 1024
        ),
    )(features, cotangent, w_self, w_neigh, bias.reshape(1, width), neighbours.T, send_rows.reshape(peers, slots).T, hub_local)


def solution(mesh):
    rows = P(("group", "dom"), None)
    return jax.shard_map(
        body,
        mesh=mesh,
        in_specs=(rows, rows, P(), P(), P(), rows, P(("group", "dom"), None, None), P(("group", "dom"))),
        out_specs=(rows, rows),
        check_vma=False,
    )
```

time: 108 us -> 98.9 us (0.916)
  Pallas kernels: 103 us -> 95.3 us
    pallas_call x1, Pallas kernels: 103 us -> 95.3 us  [body(): pl.pallas_call(functools.partial(kernel, yn, xn, zn), out_shape=(jax.Shap...]
where the time goes in v4:
time: 98.9 us; the launch traced here: 98.4 us
  Pallas kernels  95.3 us (96%)
  local copies, waits for them, and re-layouts  2.52 us (3%)
    pallas_call x1, Pallas kernels, body(): pl.pallas_call(functools.partial(kernel, yn, xn, zn), out_shape=(jax.Shap...  95.3 us
    unnamed x4, local copies, waits for them, and re-layouts  2.52 us

profile of v4, /device:TPU:6, one launch (start us, length us, event | category | flops | bytes accessed | tf_op | source)
XLA Modules:
  0.0 98.4 jit_solution(16241621633657629655)
XLA Ops:
  0.6 95.3 %shard_map.95 = (bf16[256,512]{1,0:T(8,128)(2,1)}, f32[256,512]{1,0:T(8,128)}) custom-call(bf16[256,512]{1,0:T(8,128)(2,1)} %feat_in.1, bf16[256,512]{1,0:T(8,128)(2,1)} %cot_in.1, bf16[512,512]{1,0:T(8,128)(2,1)} %ws_in.1, bf16[512,512]{1,0:T(8,128)(2,1)} %wn_in.1, f32[1,512]{1,0:T(1,128)} %bitcast.7, s32[10,256]{1,0:T(8,128)} %bitcast.5, ...), custom_call_target="tpu_custom_call" | custom-call | tf_op jit(solution)/shard_map/pallas_call | solution.py:539
  95.9 0.0 copy-start
  95.9 1.7 %copy.12 = bf16[256,512]{1,0:T(8,128)(2,1)} copy(bf16[256,512]{1,0:T(8,128)(2,1)} %get-tuple-element.4) | data formatting | bytes 524288
  97.6 0.0 copy-done
  97.6 0.8 copy.13
Async XLA Ops:
  95.9 1.7 %copy-start = (f32[256,512]{1,0:T(8,128)S(1)}, f32[256,512]{1,0:T(8,128)}, u32[]{:S(2)}) copy-start(f32[256,512]{1,0:T(8,128)} %get-tuple-element.5) | copy-start | bytes 1572868

commit v5 on v4

--- a/solution.py
+++ b/solution.py
@@ -13,22 +13,14 @@
 BF16 = jnp.bfloat16
 
 
-def dot_t(left, right):
-    return lax.dot_general(left, right, (((0,), (0,)), ((), ())), preferred_element_type=F32)
-
-
-def dot_b(left, right):
-    return lax.dot_general(left, right, (((1,), (1,)), ((), ())), preferred_element_type=F32)
-
-
 def dot(left, right):
     return jnp.dot(left, right, preferred_element_type=F32)
 
 
 def kernel(
     yn, xn, zn, feat_in, cot_in, ws_in, wn_in, bias_in, nbrt_in, sr_in, hubl, out, gout,
-    feat, cot, ws, wn, bias, nbrt, sr, lst, outv, gm,
-    tab, sel, sel_b, rel, lists, zrows, xsend, bsend, arr, gsend, gback, gback_b, zout, zin, hubtab,
+    feat, cot, ws, wn, bias, nbrt, sr, lst, gm,
+    tab, tabn, selt, wnt, wst, sel, sel_b, rel, lists, zrows, xsend, bsend, arr, gsend, gback, gback_b, zout, zin, hubtab,
     ha_s, ha, hb_s, hb, hubg, sib_s, sib, yg_s, yg, xb_s, xb, za_s, za,
     sem_z, sem_rz, sem_l, sem_x, sem_b, sem_xg, sem_gb, sem_ha, sem_hb, sem_y, sem_sib, sem_sibg, sem_yg, sem_xb, sem_za, sem_in,
 ):
@@ -123,6 +115,7 @@
         for e in range(fanout):
             total = jnp.where(nbrt[e:e + 1, :] == rows, total + 1.0, total)
         tab[pl.ds(pl.multiple_of(at, tall), tall), :] = total.astype(BF16)
+        tabn[i] = total.T.astype(BF16)
 
     tiles = tab.shape[0] // tall
     spots = 2 * hops + 1
@@ -159,14 +152,29 @@
 
     sub_id = lax.broadcasted_iota(jnp.int32, (verts, tall), 0).astype(F32)
 
-    def chosen_rows(owner, d, part, sel_at, to_at):
-        if part == 0:
-            sel_at[...] = (sub_id == lists[owner, d % zn:d % zn + 1, :].astype(F32)).astype(BF16)
-        to_at[...] = dot_t(sel_at[...], zrows[owner, part]).astype(BF16).reshape(xn, slots, cut)
-
-    def pick(j, part):
-        zz = up_z(j)
-        chosen_rows(zz, -j, part, sel.at[zz], xsend.at[zz, part])
+    def wanted_by(owner, d, sel_at, row):
+        chosen = (sub_id == lists[owner, d % zn:d % zn + 1, :].astype(F32)).astype(F32)
+        sel_at[...] = chosen.astype(BF16)
+        selt[row] = chosen.T.astype(BF16)
+
+    def prepare(way, hop):
+        side, owner = (way + 1) // 2, up_z(-way * hop)
+        wanted_by(owner, way * hop, sel.at[owner], 3 * side)
+        if hop == hops:
+            for step in (1, 2):
+                wanted_by(owner, way * (hop + step), sel_b.at[side, step - 1], 3 * side + step)
+
+    def pick(way, hop, part):
+        side, zz = (way + 1) // 2, up_z(-way * hop)
+        if hop == hops:
+            rows = dot(selt[3 * side:3 * side + 3].reshape(3 * tall, verts), zrows[zz, part]).astype(BF16)
+            for step in (1, 2):
+                bsend[side, step - 1, part] = rows[step * tall:(step + 1) * tall].reshape(xn, slots, cut)
+                send_beyond(way, step, part)
+            rows = rows[:tall]
+        else:
+            rows = dot(selt[3 * side], zrows[zz, part]).astype(BF16)
+        xsend[zz, part] = rows.reshape(xn, slots, cut)
         arr[part, zz, x] = xsend[zz, part, x]
         for i in range(1, xn):
             to = lax.rem(x + i, xn)
@@ -178,14 +186,11 @@
     def b_slot(way, step):
         return (way + 1) // 2 if step == 1 else 2
 
-    def pick_beyond(way, step, part):
+    def send_beyond(way, step, part):
         side, slot = (way + 1) // 2, 3 * part + b_slot(way, step)
-        owner = up_z(-way * hops)
-        rows = bsend.at[side, step - 1, part]
-        chosen_rows(owner, way * (hops + step), part, sel_b.at[side, step - 1], rows)
         for to in range(xn) if step == 1 else far_of(way):
             pltpu.make_async_remote_copy(
-                src_ref=rows.at[to], dst_ref=arr.at[part, owner, x],
+                src_ref=bsend.at[side, step - 1, part, to], dst_ref=arr.at[part, up_z(-way * hops), x],
                 send_sem=sem_b.at[0, slot, to], recv_sem=sem_b.at[1, slot, x],
                 device_id={"dom": to * zn + up_z(way * step)}, device_id_type=pl.DeviceIdType.MESH,
             ).start()
@@ -253,24 +258,26 @@
 
     last = 2 * hops - 1
     hub_steps = [(min(1, last), hub_z), (min(3, last), hub_x), (max(last - 1, 1), hub_y)]
+    prepare(1, 0)
     for part in range(parts):
-        pick(0, part)
+        pick(1, 0, part)
     spot = 0
     for hop in range(1, hops + 1):
         for way in (1, -1):
             send_l(way, hop).wait_recv()
             if hop < hops:
                 send_l(way, hop + 1).start()
+            prepare(way, hop)
         for part in range(parts):
             for way in (1, -1):
                 send_z(way, hop, part).wait_recv()
                 if hop < hops:
                     send_z(way, hop + 1, part).start()
                 else:
-                    pick_beyond(way, 1, part)
-                    pick_beyond(way, 2, part)
-            pick(-hop, part)
-            pick(hop, part)
+                    pick(way, hop, part)
+            if hop < hops:
+                pick(1, hop, part)
+                pick(-1, hop, part)
             if part in (parts // 2 - 1, parts - 1) and spot < last:
                 for at, step in hub_steps:
                     if at == spot:
@@ -283,13 +290,18 @@
     tally_part(spot + 1)
     hub_end()
 
+    def counts(lo, hi):
+        return jnp.concatenate([tabn[i] for i in range(lo // tall, hi // tall)], axis=1)
+
     for load in loads[3:7]:
         load.wait()
-    agg = dot_t(tab[0:verts, :], feat[...])
+    wnt[...] = wn[...].T
+    wst[...] = ws[...].T
+    agg = dot(counts(0, verts), feat[...])
     pre = dot(feat[...], ws[...]) + bias[...]
     for i in range(yn):
         send_sib(i).wait()
-    agg += dot_t(tab[hub_at:, :], hubtab[...].reshape(2 * yn * block, width))
+    agg += dot(counts(hub_at, tab.shape[0]), hubtab[...].reshape(2 * yn * block, width))
     for part in range(parts):
         cols = slice(part * cut, (part + 1) * cut)
         if xn > 1:
@@ -299,16 +311,14 @@
         for slot in range(3):
             for i in range(xn):
                 copy(bsend.at[0, 0, part, 0], arr.at[part, 0, i], sem_b, (3 * part + slot, i), **sibling).wait()
-        summed = agg[:, cols] + dot_t(tab[verts:hub_at, :], arr[part].reshape(near, cut))
+        summed = agg[:, cols] + dot(counts(verts, hub_at), arr[part].reshape(near, cut))
         pre += dot((summed / fanout).astype(BF16), wn[cols, :])
     sigm = jax.nn.sigmoid(pre)
-    outv[...] = (pre * sigm).astype(BF16)
-    store = pltpu.make_async_copy(outv, out, sem_in.at[0])
-    store.start()
     grad_pre = (cot[...].astype(F32) * sigm * (1.0 + pre * (1.0 - sigm))).astype(BF16)
-    grad_mean = (dot_b(grad_pre, wn[...]) / fanout).astype(BF16)
+    grad_mean = (dot(grad_pre, wnt[...]) / fanout).astype(BF16)
     for part in range(parts):
         gm[part] = grad_mean[:, part * cut:(part + 1) * cut]
+    out[...] = (pre * sigm).astype(BF16)
 
     def slot_grads(zz, part):
         rows = pl.ds(pl.multiple_of(verts + zz * tall, tall), tall)
@@ -391,8 +401,8 @@
         at = ((way + 1) // 2, hop, part)
         return copy(zout.at[at], zin.at[at], sem_rz, (way + 1, hop, part), **z_next[way])
 
-    def step_z(hop):
-        for way, part in turns:
+    def step_z(hop, part):
+        for way in (1, -1):
             at = (way + 1) // 2
             value = owed(way * hop, part)
             if hop < hops:
@@ -459,7 +469,7 @@
         loop(1, zn, lambda i: send_za(i).start())
 
     def self_part():
-        gout[...] = dot(tab[0:verts, :], grad_mean) + dot_b(grad_pre, ws[...])
+        gout[...] = dot(tab[0:verts, :], grad_mean) + dot(grad_pre, wst[...])
 
     def wait_sent():
         for hop in range(1, hops + 1):
@@ -469,7 +479,6 @@
             send_l(-1, hop).wait_send()
         for i in (1, -1, 2, -2, 3, -3, 4, 0):
             send_y(i).wait_send()
-        store.wait()
 
     def wait_given():
         for hop in range(2, hops + 1):
@@ -488,13 +497,19 @@
                 for to in range(xn):
                     give_beyond(side, step, slot, to, part).wait_send()
 
-    jobs = [(hops, self_part), (hops, wait_sent), (hops, relay_y), (min(2, hops), start_x), (1, end_x), (1, wait_given)]
+    end = parts - 1
+    jobs = [
+        (hops, 0, self_part), (hops, end, wait_sent), (hops - 1, 0, relay_y),
+        (min(2, hops), 0, start_x) if hops > 1 else (1, end, start_x),
+        (1, 0, end_x) if hops > 1 else (1, end, end_x), (1, end, wait_given),
+    ]
     start_y()
     for hop in range(hops, 0, -1):
-        step_z(hop)
-        for at, job in jobs:
-            if at == hop:
-                job()
+        for part in range(parts):
+            step_z(hop, part)
+            for at, when, job in jobs:
+                if (at, when) == (hop, part):
+                    job()
     for part in range(parts):
         cols = slice(part * cut, (part + 1) * cut)
         gout[:, cols] += owed(0, part)
@@ -539,11 +554,11 @@
     return pl.pallas_call(
         functools.partial(kernel, yn, xn, zn),
         out_shape=(
-            jax.ShapeDtypeStruct((verts, width), BF16),
-            jax.ShapeDtypeStruct((verts, width), F32),
+            pltpu.VMEM((verts, width), BF16),
+            pltpu.VMEM((verts, width), F32),
         ),
         in_specs=[pl.BlockSpec(memory_space=pl.ANY)] * 7 + [pl.BlockSpec(memory_space=pltpu.SMEM)],
-        out_specs=(pl.BlockSpec(memory_space=pl.ANY), vmem),
+        out_specs=(vmem, vmem),
         scratch_shapes=[
             pltpu.VMEM((verts, width), BF16),
             pltpu.VMEM((verts, width), BF16),
@@ -553,9 +568,12 @@
             pltpu.VMEM(neighbours.shape[::-1], jnp.int32),
             pltpu.VMEM((slots, peers), jnp.int32),
             pltpu.VMEM((zn, tall), F32),
-            pltpu.VMEM((verts, width), BF16),
             pltpu.VMEM((parts, verts, cut), BF16),
             pltpu.VMEM((verts + near + groups * block, verts), BF16),
+            pltpu.VMEM(((verts + near + groups * block) // tall, verts, tall), BF16),
+            pltpu.VMEM((6, tall, verts), BF16),
+            pltpu.VMEM((width, width), BF16),
+            pltpu.VMEM((width, width), BF16),
             pltpu.VMEM((zn, verts, tall), BF16),
             pltpu.VMEM((2, 2, verts, tall), BF16),
             pltpu.VMEM((16, tall), F32),
@@ -601,7 +619,7 @@
             dma((7 + parts,)),
         ],
         compiler_params=pltpu.CompilerParams(
-            collective_id=0, has_side_effects=True, vmem_limit_bytes=60 * 1024 * 1024
+            collective_id=0, has_side_effects=True, vmem_limit_bytes=63 * 1024 * 1024
         ),
     )(features, cotangent, w_self, w_neigh, bias.reshape(1, width), neighbours.T, send_rows.reshape(peers, slots).T, hub_local)
 

time: 98.9 us -> 94.8 us (0.959)
  Pallas kernels: 95.3 us -> 91.7 us
  local copies, waits for them, and re-layouts: 2.52 us -> 1.5 us
    pallas_call x1, Pallas kernels: 95.3 us -> 91.7 us  [body(): pl.pallas_call(functools.partial(kernel, yn, xn, zn), out_shape=(pltpu.VM...]
    unnamed x4 -> x2, local copies, waits for them, and re-layouts: 2.52 us -> 1.5 us
where the time goes in v5:
time: 94.8 us; the launch traced here: 93.9 us
  Pallas kernels  91.7 us (97%)
  local copies, waits for them, and re-layouts  1.5 us (2%)
    pallas_call x1, Pallas kernels, body(): pl.pallas_call(functools.partial(kernel, yn, xn, zn), out_shape=(pltpu.VM...  91.7 us

profile of v5, /device:TPU:6, one launch (start us, length us, event | category | flops | bytes accessed | tf_op | source)
XLA Modules:
  0.0 93.9 jit_solution(15496113170166590530)
XLA Ops:
  0.6 91.7 %shard_map.95 = (bf16[256,512]{1,0:T(8,128)(2,1)S(1)}, f32[256,512]{1,0:T(8,128)S(1)}) custom-call(bf16[256,512]{1,0:T(8,128)(2,1)} %feat_in.1, bf16[256,512]{1,0:T(8,128)(2,1)} %cot_in.1, bf16[512,512]{1,0:T(8,128)(2,1)} %ws_in.1, bf16[512,512]{1,0:T(8,128)(2,1)} %wn_in.1, f32[1,512]{1,0:T(1,128)} %bitcast.7, s32[10,256]{1,0:T(8,128)} %bitcast.5, ...), custom_call_target="tpu_custom_call" | custom-call | tf_op jit(solution)/shard_map/pallas_call | solution.py:554
  92.4 0.7 copy.12
  93.1 0.8 copy.13

commit v6 on v5

--- a/solution.py
+++ b/solution.py
@@ -501,7 +501,7 @@
     jobs = [
         (hops, 0, self_part), (hops, end, wait_sent), (hops - 1, 0, relay_y),
         (min(2, hops), 0, start_x) if hops > 1 else (1, end, start_x),
-        (1, 0, end_x) if hops > 1 else (1, end, end_x), (1, end, wait_given),
+        (2, end, end_x) if hops > 1 else (1, end, end_x), (1, end, wait_given),
     ]
     start_y()
     for hop in range(hops, 0, -1):

time: 94.8 us -> 93.4 us (0.985)
  no operation moved by 1% of the time
where the time goes in v6:
time: 93.4 us; the launch traced here: 93.1 us
  Pallas kernels  91 us (97%)
  local copies, waits for them, and re-layouts  1.5 us (2%)
    pallas_call x1, Pallas kernels, body(): pl.pallas_call(functools.partial(kernel, yn, xn, zn), out_shape=(pltpu.VM...  91 us

profile of v6, /device:TPU:6, one launch (start us, length us, event | category | flops | bytes accessed | tf_op | source)
XLA Modules:
  0.0 93.1 jit_solution(5870177099831977028)
XLA Ops:
  0.6 91.0 %shard_map.95 = (bf16[256,512]{1,0:T(8,128)(2,1)S(1)}, f32[256,512]{1,0:T(8,128)S(1)}) custom-call(bf16[256,512]{1,0:T(8,128)(2,1)} %feat_in.1, bf16[256,512]{1,0:T(8,128)(2,1)} %cot_in.1, bf16[512,512]{1,0:T(8,128)(2,1)} %ws_in.1, bf16[512,512]{1,0:T(8,128)(2,1)} %wn_in.1, f32[1,512]{1,0:T(1,128)} %bitcast.7, s32[10,256]{1,0:T(8,128)} %bitcast.5, ...), custom_call_target="tpu_custom_call" | custom-call | tf_op jit(solution)/shard_map/pallas_call | solution.py:554
  91.6 0.7 copy.12
  92.3 0.8 copy.13
